TPU v7x, 768 devices: a whole 4x8x12 slice. The times are simulated.
768 devices in a mesh: rows: 24 (over z_lo, x), task: 32 (over z_hi, y, core).
Axes of the slice: x: 4, y: 8, z: 12 (z_hi: 2, z_lo: 6; z = z_hi * 6 + z_lo), core: 2. Of those that a mesh axis runs over, the one named last changes fastest.
Arguments:
- hamiltonian_tiles: bfloat16 [24576, 4096], P(('rows', 'task')), may hold values from -0.1875 to 0.1875
- tile_target: int32 [24576], P(('rows', 'task')), may hold values from 0 to 767, as said below
- column_block: int32 [24576], P(('rows', 'task')), may hold values from 0 to 1535, as said below
- row_count: int32 [1536], P(('rows', 'task')), may hold values from 1 to 16
- vectors: bfloat16 [192, 98304], P('task', 'rows'), may hold values from -6 to 6
- expansion_coef: float32 [5], replicated, may hold values from -3 to 3
Outputs:
- fermi_vectors: bfloat16 [192, 98304], P('task', 'rows')
Inputs may be any that keep to these rules, and one draw needn't show every extreme that they name: `tile_target`: for each task index, the values on the 24 devices of that task index together are each of 0 to 767 once; a device sends none or exactly 2 of its blocks to any device of the rows axis. `column_block`: slot 0 of block row g names column block g; the other slots name column blocks within 8 of g, distinct except near the matrix's ends, where the numbers are cut to 0 and 1535 and may repeat.
All inputs are finite; a program needn't handle non-finite values.
Results may differ from a plain program's by a relative error of at most 0.013.
Values may be sent and summed in bfloat16 or wider, within the bound.
A program may use at most 64 MiB of HBM per device.

v0:
```python
import jax
import jax.numpy as jnp
from jax import lax
from jax.sharding import PartitionSpec as P

TILE = 64
SLOTS_ROW = 16
REACH = 8
ITERS = 4


def padded_2(block, sides, width):
    for axis, dim in sides:
        count = lax.axis_size(axis)
        forward = [(i, i + 1) for i in range(count - 1)]
        backward = [(target, source) for source, target in forward]
        low = lax.ppermute(
            lax.slice_in_dim(block, block.shape[dim] - width, None, axis=dim), axis, forward
        )
        high = lax.ppermute(lax.slice_in_dim(block, 0, width, axis=dim), axis, backward)
        block = jnp.concatenate([low, block, high], axis=dim)
    return block


def local(hamiltonian_tiles, tile_target, column_block, row_count, vectors, expansion_coef):
    slots_dev = hamiltonian_tiles.shape[0]
    tile_len = hamiltonian_tiles.shape[1]
    row_groups = lax.axis_size("rows")
    block_rows = row_count.shape[0]
    capacity = max(2, slots_dev // min(row_groups, 16))
    owners = tile_target // slots_dev
    labels = tile_target % slots_dev
    position = jnp.arange(slots_dev, dtype=jnp.int32)
    earlier = (owners[:, None] == owners[None, :]) & (position[None, :] < position[:, None])
    slot_of = owners * capacity + jnp.sum(earlier.astype(jnp.int32), axis=1)
    outgoing = (
        jnp.zeros((row_groups * capacity, tile_len), jnp.bfloat16)
        .at[slot_of]
        .set(hamiltonian_tiles)
    )
    out_labels = jnp.full((row_groups * capacity,), slots_dev, jnp.int32).at[slot_of].set(labels)
    arrived, arrived_labels = (
        lax.all_to_all(outgoing, "rows", split_axis=0, concat_axis=0, tiled=True),
        lax.all_to_all(out_labels, "rows", split_axis=0, concat_axis=0, tiled=True),
    )
    placed = (
        jnp.zeros((slots_dev + 1, tile_len), jnp.bfloat16)
        .at[arrived_labels]
        .set(arrived)[:slots_dev]
    )
    live = (position % SLOTS_ROW < jnp.repeat(row_count, SLOTS_ROW)).astype(jnp.bfloat16)
    placed = placed * live[:, None]
    rim_rows = REACH * TILE
    panel_len = vectors.shape[1]
    panel_blocks = panel_len // TILE
    first_block = lax.axis_index("rows") * panel_blocks - REACH
    tiles = placed.reshape(block_rows, SLOTS_ROW, TILE, TILE)
    local_cols = column_block - first_block

    def apply_matrix(current):
        padded = padded_2(current, (("rows", 1),), rim_rows)
        piece = lax.all_gather(padded, "task", axis=0, tiled=True)
        how_many = piece.shape[0]
        picked = piece.reshape(how_many, -1, TILE)[:, local_cols, :].reshape(
            how_many, block_rows, SLOTS_ROW, TILE
        )
        result = jnp.einsum("nikb,ikab->nia", picked, tiles, preferred_element_type=jnp.float32)
        mine = result.reshape(how_many, block_rows * TILE)
        return lax.all_to_all(mine, "task", split_axis=0, concat_axis=1, tiled=True)

    previous = vectors
    total = expansion_coef[0] * vectors.astype(jnp.float32)
    current = apply_matrix(vectors).astype(jnp.bfloat16)
    total = total + expansion_coef[1] * current.astype(jnp.float32)
    for order in range(2, ITERS + 1):
        product = apply_matrix(current)
        following = (2.0 * product - previous.astype(jnp.float32)).astype(jnp.bfloat16)
        total = total + expansion_coef[order] * following.astype(jnp.float32)
        previous, current = (current, following)
    result = total.astype(jnp.bfloat16)
    return result


def solution(mesh):
    in_specs = (
        P(("rows", "task"), None),
        P(("rows", "task")),
        P(("rows", "task")),
        P(("rows", "task")),
        P("task", "rows"),
        P(),
    )
    out_specs = P("task", "rows")
    return jax.shard_map(local, mesh=mesh, in_specs=in_specs, out_specs=out_specs, check_vma=False)
```

profile of v0, /device:TPU:6, one launch (start us, length us, event | category | flops | bytes accessed | tf_op | source)
XLA Modules:
  0.0 645.5 jit_solution(12124199373381186569)
XLA Ops:
  7.3 4.2 collective-permute-start
  11.4 1.9 collective-permute-start.1
  13.4 5.7 collective-permute-done.1
  19.1 1.5 maximum_bitcast_fusion
  22.8 13.0 %all-to-all-start = ((s32[24,2,1]{1,2,0:T(1,128)}), s32[24,2,1]{1,2,0:T(1,128)S(1)}, u32[]{:S(2)}, u32[]{:S(2)}) async-start(s32[24,2,1]{1,2,0:T(1,128)} %bitcast.2), calls=%async_computation | async-start | bytes 24576 | tf_op jit(solution)/shard_map/all_to_all | solution.py:44
  35.9 1.5 scatter_custom_fusion.1
  37.4 1.0 all_to_all.59
  38.4 6.3 all-to-all-done
  44.7 5.7 all-to-all-start.1
  50.4 0.7 broadcast_in_dim.32
  53.2 14.9 %all-to-all-done.1 = bf16[24,2,4096]{2,1,0:T(2,128)(2,1)S(1)} async-done(((bf16[24,2,4096]{2,1,0:T(2,128)(2,1)}), bf16[24,2,4096]{2,1,0:T(2,128)(2,1)S(1)}, u32[]{:S(2)}, u32[]{:S(2)}) %all-to-all-start.1) | async-done | bytes 393248 | tf_op jit(solution)/shard_map/all_to_all | solution.py:43
  68.2 1.2 scatter_custom_fusion.2
  70.1 70.5 %all-gather.9.cloned.1.call-done = bf16[32,6,5120]{2,1,0:T(8,128)(2,1)} async-done(((bf16[1,6,5120]{2,1,0:T(8,128)(2,1)}), bf16[32,6,5120]{2,1,0:T(8,128)(2,1)}) %all-gather.9.cloned.1.call-update) | async-done | bytes 1966096 | tf_op jit(solution)/shard_map/all_gather | solution.py:62
  140.6 6.3 reshape.108
  146.9 5.3 copy.33
  152.3 1.6 gather_fusion
  153.9 1.5 convolution_bitcast_fusion.3
  155.7 19.2 %all_to_all.76 = bf16[32,6,128]{2,1,0:T(8,128)(2,1)S(1)} all-to-all(bf16[32,6,128]{2,1,0:T(8,128)(2,1)S(1)} %all_to_all.62), channel_id=1, replica_groups=mesh['rows'=24,'task'=32] {'task'}, dimensions={0} | all-to-all | bytes 98304 | tf_op jit(solution)/shard_map/all_to_all | solution.py:69
  174.9 2.8 collective-permute-start.2
  177.7 3.0 collective-permute-start.3
  180.7 4.6 collective-permute-done.3
  186.0 106.3 %all-gather.11.cloned.1.call-done = bf16[32,6,5120]{2,1,0:T(8,128)(2,1)} async-done(((bf16[1,6,5120]{2,1,0:T(8,128)(2,1)}), bf16[32,6,5120]{2,1,0:T(8,128)(2,1)}) %all-gather.11.cloned.1.call-update) | async-done | bytes 1966096 | tf_op jit(solution)/shard_map/all_gather | solution.py:62
  292.4 6.3 reshape.110
  298.7 5.3 copy.35
  304.1 1.6 gather_fusion.1
  305.7 1.5 convolution_bitcast_fusion.2
  307.5 19.9 %all_to_all.77 = f32[32,6,128]{2,1,0:T(8,128)S(1)} all-to-all(f32[32,6,128]{2,1,0:T(8,128)S(1)} %all_to_all.64), channel_id=1, replica_groups=mesh['rows'=24,'task'=32] {'task'}, dimensions={0} | all-to-all | bytes 196608 | tf_op jit(solution)/shard_map/all_to_all | solution.py:69
  327.4 2.6 collective-permute-start.4
  330.1 3.2 collective-permute-start.5
  333.3 4.4 collective-permute-done.5
  338.4 107.4 %all-gather.13.cloned.1.call-done = bf16[32,6,5120]{2,1,0:T(8,128)(2,1)} async-done(((bf16[1,6,5120]{2,1,0:T(8,128)(2,1)}), bf16[32,6,5120]{2,1,0:T(8,128)(2,1)}) %all-gather.13.cloned.1.call-update) | async-done | bytes 1966096 | tf_op jit(solution)/shard_map/all_gather | solution.py:62
  445.8 6.3 reshape.112
  452.1 5.3 copy.37
  457.5 1.6 gather_fusion.2
  459.1 1.5 convolution_bitcast_fusion.1
  461.0 19.9 %all_to_all.78 = f32[32,6,128]{2,1,0:T(8,128)S(1)} all-to-all(f32[32,6,128]{2,1,0:T(8,128)S(1)} %all_to_all.66), channel_id=1, replica_groups=mesh['rows'=24,'task'=32] {'task'}, dimensions={0} | all-to-all | bytes 196608 | tf_op jit(solution)/shard_map/all_to_all | solution.py:69
  480.8 2.6 collective-permute-start.6
  483.5 3.4 collective-permute-start.7
  486.9 4.2 collective-permute-done.7
  491.8 107.4 %all-gather.15.cloned.1.call-done = bf16[32,6,5120]{2,1,0:T(8,128)(2,1)} async-done(((bf16[1,6,5120]{2,1,0:T(8,128)(2,1)}), bf16[32,6,5120]{2,1,0:T(8,128)(2,1)}) %all-gather.15.cloned.1.call-update) | async-done | bytes 1966096 | tf_op jit(solution)/shard_map/all_gather | solution.py:62
  599.2 6.3 reshape.114
  605.6 5.3 copy.39
  610.9 1.6 gather_fusion.3
  612.5 1.5 convolution_bitcast_fusion
  614.2 0.8 all_to_all.68
  615.0 4.4 all-to-all-start.5
  620.2 14.9 %all-to-all-done.5 = f32[32,6,128]{2,1,0:T(8,128)S(1)} async-done(((f32[32,6,128]{2,1,0:T(8,128)}), f32[32,6,128]{2,1,0:T(8,128)S(1)}, u32[]{:S(2)}, u32[]{:S(2)}) %all-to-all-start.5) | async-done | bytes 98336 | tf_op jit(solution)/shard_map/all_to_all | solution.py:69
  635.1 3.8 fusion.8
  (49 shorter events, 9.6 us)
Async XLA Ops:
  6.5 134.1 %all-gather.9.cloned.1.call-start = ((), (), s32[]{:S(2)}) async-start(), calls=%async_computation.6 | async-start | bytes 2703360 | tf_op jit(solution)/shard_map/all_gather | solution.py:62
  7.3 6.1 collective-permute-start
  11.4 7.7 %collective-permute-start.1 = (bf16[6,512]{1,0:T(8,128)(2,1)S(1)}, bf16[6,512]{1,0:T(8,128)(2,1)S(1)}, u32[]{:S(2)}, u32[]{:S(2)}) collective-permute-start(bf16[6,512]{1,0:T(8,128)(2,1)S(1)} %get-tuple-element.12), channel_id=1, source_target_pairs={{32,0},{64,32},{96,64},{128,96},{160,128},{192,160},{224,192},{256... | collective-permute-start | bytes 18440 | tf_op jit(solution)/shard_map/ppermute | solution.py:20
  22.8 21.8 %all-to-all-start = ((s32[24,2,1]{1,2,0:T(1,128)}), s32[24,2,1]{1,2,0:T(1,128)S(1)}, u32[]{:S(2)}, u32[]{:S(2)}) async-start(s32[24,2,1]{1,2,0:T(1,128)} %bitcast.2), calls=%async_computation | async-start | bytes 24576 | tf_op jit(solution)/shard_map/all_to_all | solution.py:44
  44.7 23.4 %all-to-all-start.1 = ((bf16[24,2,4096]{2,1,0:T(2,128)(2,1)}), bf16[24,2,4096]{2,1,0:T(2,128)(2,1)S(1)}, u32[]{:S(2)}, u32[]{:S(2)}) async-start(bf16[24,2,4096]{2,1,0:T(2,128)(2,1)} %all_to_all.59), calls=%async_computation.1 | async-start | bytes 786432 | tf_op jit(solution)/shard_map/all_to_all | solution.py:43
  50.3 242.0 %all-gather.11.cloned.1.call-start = ((), (), s32[]{:S(2)}) async-start(), calls=%async_computation.7 | async-start | bytes 2703360 | tf_op jit(solution)/shard_map/all_gather | solution.py:62
  174.9 5.8 collective-permute-start.2
  177.7 7.7 %collective-permute-start.3 = (bf16[6,512]{1,0:T(8,128)(2,1)S(1)}, bf16[6,512]{1,0:T(8,128)(2,1)S(1)}, u32[]{:S(2)}, u32[]{:S(2)}) collective-permute-start(bf16[6,512]{1,0:T(8,128)(2,1)S(1)} %get-tuple-element.10), channel_id=1, source_target_pairs={{32,0},{64,32},{96,64},{128,96},{160,128},{192,160},{224,192},{256... | collective-permute-start | bytes 18440 | tf_op jit(solution)/shard_map/ppermute | solution.py:20
  186.0 259.8 %all-gather.13.cloned.1.call-start = ((), (), s32[]{:S(2)}) async-start(), calls=%async_computation.8 | async-start | bytes 2703360 | tf_op jit(solution)/shard_map/all_gather | solution.py:62
  304.1 23.3 %copy-start = (bf16[6,4096]{1,0:T(8,128)(2,1)S(1)}, bf16[6,4096]{1,0:T(8,128)(2,1)}, u32[]{:S(2)}) copy-start(bf16[6,4096]{1,0:T(8,128)(2,1)} %param.10) | copy-start | bytes 147460
  327.4 5.9 collective-permute-start.4
  330.1 7.7 %collective-permute-start.5 = (bf16[6,512]{1,0:T(8,128)(2,1)S(1)}, bf16[6,512]{1,0:T(8,128)(2,1)S(1)}, u32[]{:S(2)}, u32[]{:S(2)}) collective-permute-start(bf16[6,512]{1,0:T(8,128)(2,1)S(1)} %get-tuple-element.8), channel_id=1, source_target_pairs={{32,0},{64,32},{96,64},{128,96},{160,128},{192,160},{224,192},{256... | collective-permute-start | bytes 18440 | tf_op jit(solution)/shard_map/ppermute | solution.py:20
  338.4 260.8 %all-gather.15.cloned.1.call-start = ((), (), s32[]{:S(2)}) async-start(), calls=%async_computation.9 | async-start | bytes 2703360 | tf_op jit(solution)/shard_map/all_gather | solution.py:62
  480.8 6.0 collective-permute-start.6
  483.5 7.7 %collective-permute-start.7 = (bf16[6,512]{1,0:T(8,128)(2,1)S(1)}, bf16[6,512]{1,0:T(8,128)(2,1)S(1)}, u32[]{:S(2)}, u32[]{:S(2)}) collective-permute-start(bf16[6,512]{1,0:T(8,128)(2,1)S(1)} %get-tuple-element.6), channel_id=1, source_target_pairs={{32,0},{64,32},{96,64},{128,96},{160,128},{192,160},{224,192},{256... | collective-permute-start | bytes 18440 | tf_op jit(solution)/shard_map/ppermute | solution.py:20
  610.9 8.6 %copy-start.1 = (f32[5]{0:T(128)S(1)}, f32[5]{0:T(128)}, u32[]{:S(2)}) copy-start(f32[5]{0:T(128)} %param.11) | copy-start | bytes 64
  615.0 20.1 %all-to-all-start.5 = ((f32[32,6,128]{2,1,0:T(8,128)}), f32[32,6,128]{2,1,0:T(8,128)S(1)}, u32[]{:S(2)}, u32[]{:S(2)}) async-start(f32[32,6,128]{2,1,0:T(8,128)} %all_to_all.68), calls=%async_computation.5 | async-start | bytes 262144 | tf_op jit(solution)/shard_map/all_to_all | solution.py:69
Sparse Core Ops, SparseCore 0:
  20.7 119.8 all-gather.8
  186.1 106.2 all-gather.10
  338.5 107.2 all-gather.12
  491.9 107.2 all-gather.14
where the time goes:
time: 648 us; the launch traced here: 645 us
  waiting for transfers between devices  447 us (69%)
  local copies, waits for them, and re-layouts  63.5 us (10%)
  blocking collectives  58.9 us (9%)
  starting transfers between devices  47.1 us (7%)
  between operations  13.5 us (2%)
  other arithmetic  9.54 us (1%)
    all_gather x4, waiting for transfers between devices, apply_matrix(): piece = lax.all_gather(padded, 'task', axis=0, tiled=True)  392 us
    all_to_all x3, blocking collectives, apply_matrix(): return lax.all_to_all(mine, 'task', split_axis=0, concat_axis=1, tiled=True)  58.9 us
    reshape x8, local copies, waits for them, and re-layouts, apply_matrix(): piece.reshape(how_many, -1, TILE)[:, local_cols, :]  46.7 us
    ppermute x4, waiting for transfers between devices, padded_2(): lax.ppermute(lax.slice_in_dim(block, 0, width, axis=dim), axis, backward)  19 us
    all_to_all x1, waiting for transfers between devices, apply_matrix(): return lax.all_to_all(mine, 'task', split_axis=0, concat_axis=1, tiled=True)  14.9 us
    all_to_all x1, waiting for transfers between devices, local(): lax.all_to_all(outgoing, 'rows', split_axis=0, concat_axis=0, tiled=True)  14.9 us
    all_to_all x1, starting transfers between devices, local(): lax.all_to_all(out_labels, 'rows', split_axis=0, concat_axis=0, tiled=True)  13 us
  transfers between devices with their start and end apart: 15, of which 11 were waited for; matrix products, arithmetic and copies ran while one was open for 1% of the time, Pallas kernels for 0%

commit v1 on v0

v1 whole, which is shorter than its diff:
```python
import jax
import jax.numpy as jnp
from jax import lax
from jax.experimental import pallas as pl
from jax.experimental.pallas import tpu as pltpu
from jax.sharding import PartitionSpec as P

TILE = 64
SLOTS_ROW = 16
REACH = 8
ITERS = 4
MESH = pl.DeviceIdType.MESH
F32 = jnp.float32
BF16 = jnp.bfloat16

N_ROWS = 24
N_TASK = 32
CHIPS = 384
CHIP_ROWS = 4
WINDOW = 5
OWN = 2
MINE = 6
PAD = 8
SOURCES = 16
HALF_VECTORS = MINE * SOURCES
WIDTH = CHIP_ROWS * TILE


def place(half, y, core):
    z = lax.div(half, 4)
    x = lax.rem(half - z, 4)
    return lax.rem(z, 6) * 4 + x, lax.div(z, 6) * 16 + y * 2 + core


def one_hot(condition):
    return jnp.where(condition, 1.0, 0.0).astype(BF16)


def iota(shape, dim):
    return lax.broadcasted_iota(jnp.int32, shape, dim)


def kernel(
    tiles_ref, meta_ref, info_ref, vec_ref, coef_ref, out_ref,
    send_h, recv_h, send_lab, recv_lab, recv_info, send_v, recv_v,
    band_raw, band, win, total, send_f, recv_f,
    h_send, lab_send, v_send, one_send, rim_send, f_send,
    h_recv, lab_recv, v_recv, info_recv, band_recv, rim_recv, f_recv,
):
    row, task = lax.axis_index("rows"), lax.axis_index("task")
    zh, y, core = lax.div(task, 16), lax.rem(lax.div(task, 2), 8), lax.rem(task, 2)
    z, x = zh * 6 + lax.div(row, 4), lax.rem(row, 4)
    half = 4 * z + lax.rem(x + z, 4)
    chip = half * 8 + y

    def transfer(src, dst, send_sem, recv_sem, where):
        to_row, to_task = where
        here = (to_row == row) & (to_task == task)

        @pl.when(here)
        def _():
            pltpu.make_async_copy(src, dst, recv_sem).start()

        @pl.when(jnp.logical_not(here))
        def _():
            pltpu.make_async_remote_copy(
                src, dst, send_sem, recv_sem, device_id=where, device_id_type=MESH
            ).start()

    def sent(src, send_sem, recv_sem, where):
        to_row, to_task = where

        @pl.when(jnp.logical_not((to_row == row) & (to_task == task)))
        def _():
            pltpu.make_async_remote_copy(
                src, src, send_sem, recv_sem, device_id=where, device_id_type=MESH
            ).wait_send()

    def arrived(buffer, sem):
        pltpu.make_async_copy(buffer, buffer, sem).wait()

    slot_v = zh * 8 + y

    def vector_owner(p):
        return place(2 * row + lax.div(p, 8), lax.rem(p, 8), core)

    mine = vec_ref[...].astype(F32)
    for p in range(SOURCES):
        left = mine[:, p * WIDTH : p * WIDTH + 128]
        right = mine[:, p * WIDTH + 128 : (p + 1) * WIDTH]
        send_v[p] = jnp.concatenate([left, right], axis=0).astype(BF16)

    @pl.loop(0, SOURCES)
    def _(p):
        transfer(send_v.at[p], recv_v.at[slot_v], v_send.at[p], v_recv, vector_owner(p))

    info_owner = place(2 * row + zh, y, core)
    transfer(info_ref, recv_info, one_send.at[0], info_recv, info_owner)

    slots, names = meta_ref[0:1, :], meta_ref[1:2, :]
    place_row = lax.shift_right_logical(iota((N_ROWS * 8, 128), 0), 3)
    pair = [
        jnp.sum(
            jnp.where(slots[:, :128] == (2 * place_row + s) * 8, names[:, :128], 0).astype(F32),
            axis=1,
            keepdims=True,
        )
        for s in range(2)
    ]
    second = (iota((N_ROWS * 8, 128), 1) & 8) > 0
    send_lab[...] = (jnp.where(second, pair[1], pair[0]) - 1.0).reshape(N_ROWS, 8, 128)

    stacked = jnp.concatenate([tiles_ref[:, u * 512 : (u + 1) * 512] for u in range(8)], axis=0)
    packing = one_hot(iota((N_ROWS * 16, 256), 0) == slots)
    packed = jnp.dot(packing, stacked, preferred_element_type=F32)
    send_h[...] = packed.astype(BF16).reshape(N_ROWS, 16, 512)

    def block_owner(to):
        return place(2 * to + zh, y, core)

    @pl.loop(0, N_ROWS)
    def _(k):
        to = lax.rem(row + k, N_ROWS)
        where = block_owner(to)
        transfer(send_lab.at[to], recv_lab.at[row], lab_send.at[to], lab_recv, where)
        transfer(send_h.at[to], recv_h.at[row], h_send.at[to], h_recv, where)

    arrived(recv_v, v_recv)
    pieces = recv_v[...].reshape(SOURCES * 16, 128)

    def selector(shape, vector_dim, side):
        where = iota(shape, 1 - vector_dim)
        lane = where & 7
        vector = lax.shift_right_logical(where, 4) * MINE + lane
        fits = (lane < MINE) & ((where & 8) == 8 * side)
        return one_hot((iota(shape, vector_dim) == vector) & fits)

    for side in range(2):
        pick = selector((HALF_VECTORS, SOURCES * 16), 0, side)
        got = jnp.dot(pick, pieces, preferred_element_type=F32)
        win[0, OWN, :, side * 128 : (side + 1) * 128] = got.astype(BF16)

    def rim(step, away):
        other = lax.rem(chip + away + CHIPS, CHIPS)
        where = place(lax.div(other, 8), lax.rem(other, 8), core)
        index = away + 2 if away < 0 else away + 1
        return pltpu.make_async_remote_copy(
            win.at[step, OWN],
            win.at[step, OWN - away],
            rim_send.at[step, index],
            rim_recv.at[step, OWN - away],
            device_id=where,
            device_id_type=MESH,
        )

    def send_rims(step):
        for away in (-2, 2, -1, 1):
            rim(step, away).start()

    send_rims(0)
    total[...] = coef_ref[0] * win[0, OWN].astype(F32)

    arrived(recv_info, info_recv)
    arrived(recv_lab, lab_recv)
    wide = (N_ROWS * 8, N_ROWS * 16)
    lab = recv_lab[...].reshape(N_ROWS * 8, 128)
    lab = jnp.concatenate([lab] * 3, axis=1)
    keep = iota(wide, 0) == lax.shift_right_logical(iota(wide, 1), 4) * 8
    lab = jnp.sum(jnp.where(keep, lab, 0.0), axis=0, keepdims=True)
    info = jnp.concatenate([recv_info[...]] * 3, axis=1)
    at_slot = iota((32, N_ROWS * 16), 0).astype(F32) == lab
    code = jnp.sum(jnp.where(at_slot, info, 0.0), axis=0, keepdims=True) - 1.0
    goes = code * 8.0 + (iota((1, N_ROWS * 16), 1) & 7).astype(F32)
    columns = WINDOW * CHIP_ROWS
    placing = one_hot(iota((columns * 16, N_ROWS * 16), 0).astype(F32) == goes)

    arrived(recv_h, h_recv)
    blocks = recv_h[...].reshape(N_ROWS * 16, 512)
    raw = jnp.dot(placing, blocks, preferred_element_type=F32)
    low = iota((16, 128), 1) < TILE
    for pair_at in range(columns // 2):
        for group in range(4):
            lanes = slice(group * 128, (group + 1) * 128)
            a = raw[pair_at * 32 : pair_at * 32 + 16, lanes]
            b = raw[pair_at * 32 + 16 : pair_at * 32 + 32, lanes]
            even = jnp.where(low, a, pltpu.roll(b, TILE, 1))
            odd = jnp.where(low, pltpu.roll(a, TILE, 1), b)
            to = slice(pair_at * 128, (pair_at + 1) * 128)
            band_raw[group * 32 : group * 32 + 16, to] = even.astype(BF16)
            band_raw[group * 32 + 16 : group * 32 + 32, to] = odd.astype(BF16)
    at = iota((128, 128), 0)
    inner = lax.shift_right_logical(at, 3) & 7
    source = (at & 7) * 16 + lax.shift_right_logical(at, 6) * 8 + inner
    turn = one_hot(iota((128, 128), 1) == source)
    mine_rows = pl.ds(pl.multiple_of(core * 128, 128), 128)
    band[mine_rows, :] = jnp.dot(turn, band_raw[...], preferred_element_type=F32).astype(BF16)
    sibling = pltpu.make_async_remote_copy(
        band.at[mine_rows],
        band.at[mine_rows],
        one_send.at[1],
        band_recv,
        device_id=(row, task + 1 - 2 * core),
        device_id_type=MESH,
    )
    sibling.start()
    sibling.wait_recv()

    for step in range(ITERS):
        product = None
        for j in (OWN, 1, 3, 0, 4):
            if j != OWN:
                rim(step, OWN - j).wait_recv()
            term = lax.dot_general(
                win[step, j],
                band[:, j * WIDTH : (j + 1) * WIDTH],
                (((1,), (1,)), ((), ())),
                preferred_element_type=F32,
            )
            product = term if product is None else product + term
        if step:
            product = 2.0 * product - win[step - 1, OWN].astype(F32)
        current = product.astype(BF16)
        if step < ITERS - 1:
            win[step + 1, OWN] = current
            send_rims(step + 1)
        total[...] += coef_ref[step + 1] * current.astype(F32)

    result = total[...].astype(BF16)
    spread = None
    for side in range(2):
        put = selector((SOURCES * 16, HALF_VECTORS), 1, side)
        part = jnp.dot(put, result[:, side * 128 : (side + 1) * 128], preferred_element_type=F32)
        spread = part if spread is None else spread + part
    send_f[...] = spread.astype(BF16).reshape(SOURCES, 16, 128)
    slot_f = lax.rem(half, 2) * 8 + y

    def result_owner(q):
        return lax.div(half, 2), lax.div(q, 8) * 16 + lax.rem(q, 8) * 2 + core

    @pl.loop(0, SOURCES)
    def _(q):
        transfer(send_f.at[q], recv_f.at[slot_f], f_send.at[q], f_recv, result_owner(q))

    @pl.loop(0, N_ROWS)
    def _(to):
        where = block_owner(to)
        sent(send_lab.at[to], lab_send.at[to], lab_recv, where)
        sent(send_h.at[to], h_send.at[to], h_recv, where)

    @pl.loop(0, SOURCES)
    def _(p):
        sent(send_v.at[p], v_send.at[p], v_recv, vector_owner(p))
        sent(send_f.at[p], f_send.at[p], f_recv, result_owner(p))

    sent(info_ref, one_send.at[0], info_recv, info_owner)
    sibling.wait_send()
    for step in range(ITERS):
        for away in (-2, 2, -1, 1):
            rim(step, away).wait_send()

    arrived(recv_f, f_recv)
    final = recv_f[...].astype(F32)
    flat = [final[p, 8 * s : 8 * s + 8, :] for p in range(SOURCES) for s in range(2)]
    out_ref[...] = jnp.concatenate(flat, axis=1).astype(BF16)[:MINE, :]


def local(hamiltonian_tiles, tile_target, column_block, row_count, vectors, expansion_coef):
    slots_dev = hamiltonian_tiles.shape[0]
    position = jnp.arange(slots_dev, dtype=jnp.int32)
    owners = tile_target // slots_dev
    earlier = (owners[:, None] == owners[None, :]) & (position[None, :] < position[:, None])
    slot_of = owners * 2 + jnp.sum(earlier.astype(jnp.int32), axis=1)
    slots = (slot_of[None, :] * 8 + jnp.arange(8, dtype=jnp.int32)[:, None]).reshape(1, -1)
    names = jnp.pad(tile_target % slots_dev + 1, (0, 256 - slots_dev))[None, :]
    meta = jnp.concatenate([slots, names], axis=0)
    device = lax.axis_index("rows") * N_TASK + lax.axis_index("task")
    first = (device // 2 - OWN) * CHIP_ROWS
    owner_row = position // SLOTS_ROW
    live = (position % SLOTS_ROW).reshape(2, SLOTS_ROW) < row_count[:, None]
    code = (column_block - first) * 2 + owner_row + 1
    code = jnp.where(live.reshape(-1), code, 0).astype(F32)
    info = jnp.broadcast_to(code[:, None], (slots_dev, 128))
    padded = jnp.pad(vectors, ((0, PAD - MINE), (0, 0)))
    dma = pltpu.SemaphoreType.DMA
    vmem = pl.BlockSpec(memory_space=pltpu.VMEM)
    return pl.pallas_call(
        kernel,
        out_shape=jax.ShapeDtypeStruct(vectors.shape, BF16),
        in_specs=[vmem] * 4 + [pl.BlockSpec(memory_space=pltpu.SMEM)],
        out_specs=vmem,
        scratch_shapes=[
            pltpu.VMEM((N_ROWS, 16, 512), BF16),
            pltpu.VMEM((N_ROWS, 16, 512), BF16),
            pltpu.VMEM((N_ROWS, 8, 128), F32),
            pltpu.VMEM((N_ROWS, 8, 128), F32),
            pltpu.VMEM((32, 128), F32),
            pltpu.VMEM((SOURCES, 16, 128), BF16),
            pltpu.VMEM((SOURCES, 16, 128), BF16),
            pltpu.VMEM((128, WINDOW * WIDTH), BF16),
            pltpu.VMEM((WIDTH, WINDOW * WIDTH), BF16),
            pltpu.VMEM((ITERS, WINDOW, HALF_VECTORS, WIDTH), BF16),
            pltpu.VMEM((HALF_VECTORS, WIDTH), F32),
            pltpu.VMEM((SOURCES, 16, 128), BF16),
            pltpu.VMEM((SOURCES, 16, 128), BF16),
            dma((N_ROWS,)),
            dma((N_ROWS,)),
            dma((SOURCES,)),
            dma((2,)),
            dma((ITERS, 4)),
            dma((SOURCES,)),
            dma(()),
            dma(()),
            dma(()),
            dma(()),
            dma(()),
            dma((ITERS, WINDOW)),
            dma(()),
        ],
        compiler_params=pltpu.CompilerParams(
            has_side_effects=True, vmem_limit_bytes=32 * 1024 * 1024
        ),
    )(hamiltonian_tiles, meta, info, padded, expansion_coef)


def solution(mesh):
    in_specs = (
        P(("rows", "task"), None),
        P(("rows", "task")),
        P(("rows", "task")),
        P(("rows", "task")),
        P("task", "rows"),
        P(),
    )
    out_specs = P("task", "rows")
    return jax.shard_map(local, mesh=mesh, in_specs=in_specs, out_specs=out_specs, check_vma=False)
```

time: 648 us -> 93.1 us (0.14)
  waiting for transfers between devices: 447 us -> 0 us
  Pallas kernels: 0 us -> 87.3 us
  local copies, waits for them, and re-layouts: 63.5 us -> 3.23 us
  blocking collectives: 58.9 us -> 0 us
  starting transfers between devices: 47.1 us -> 0 us
  between operations: 13.5 us -> 0.03 us
  other arithmetic: 9.54 us -> 1.53 us
    all_gather x4 -> x0, waiting for transfers between devices: 392 us -> none  [apply_matrix(): piece = lax.all_gather(padded, 'task', axis=0, tiled=True)]
    pallas_call x0 -> x1, Pallas kernels: none -> 87.3 us  [local(): pl.pallas_call(kernel, out_shape=jax.ShapeDtypeStruct(vectors.shape, BF16...]
    all_to_all x3 -> x0, blocking collectives: 58.9 us -> none  [apply_matrix(): return lax.all_to_all(mine, 'task', split_axis=0, concat_axis=1, tiled=True)]
    reshape x10 -> x0, local copies, waits for them, and re-layouts: 47.3 us -> none  [the longest x8 46.7 us: apply_matrix(): piece.reshape(how_many, -1, TILE)[:, local_cols, :]]
    all_to_all x3 -> x0, waiting for transfers between devices: 36.1 us -> none  [the longest x1 14.9 us: apply_matrix(): return lax.all_to_all(mine, 'task', split_axis=0, concat_axis=1, tiled=True)]
    ppermute x8 -> x0, starting transfers between devices: 23.8 us -> none  [the longest x4 12.2 us: padded_2(): lax.ppermute(lax.slice_in_dim(block, block.shape[dim] - width, None, axis...]
    all_to_all x3 -> x0, starting transfers between devices: 23.1 us -> none  [the longest x1 13 us: local(): lax.all_to_all(out_labels, 'rows', split_axis=0, concat_axis=0, tiled=True)]
    ppermute x8 -> x0, waiting for transfers between devices: 19 us -> none  [the longest x4 19 us: padded_2(): lax.ppermute(lax.slice_in_dim(block, 0, width, axis=dim), axis, backward)]
  transfers between devices with their start and end apart: 15 -> 0, of which waited for: 11 -> 0; matrix products, arithmetic and copies ran while one was open for 1% -> 0% of each run, Pallas kernels for 0% -> 0%
where the time goes in v1:
time: 93.1 us; the launch traced here: 92.1 us
  Pallas kernels  87.3 us (94%)
  local copies, waits for them, and re-layouts  3.23 us (3%)
  other arithmetic  1.53 us (2%)
    pallas_call x1, Pallas kernels, local(): pl.pallas_call(kernel, out_shape=jax.ShapeDtypeStruct(vectors.shape, BF16...  87.3 us
    unnamed x7, local copies, waits for them, and re-layouts  2.22 us

profile of v1, /device:TPU:6, one launch (start us, length us, event | category | flops | bytes accessed | tf_op | source)
XLA Modules:
  0.0 92.1 jit_solution(14819476756052341433)
XLA Ops:
  0.0 0.0 copy-start.2
  0.0 0.8 lt.39
  0.8 0.1 lt.40
  0.8 0.7 fusion.3
  1.5 0.7 and_select_fusion.3
  2.2 0.2 convert_reduce_fusion
  2.4 0.1 add.62
  2.5 0.1 broadcast_in_dim.6.info_ref
  2.5 0.0 copy-done.2
  2.5 0.0 copy-start.1
  2.6 0.6 copy-done.1
  3.2 0.0 copy-start
  3.2 0.9 %copy-done = bf16[32,4096]{1,0:T(8,128)(2,1)S(1)} copy-done((bf16[32,4096]{1,0:T(8,128)(2,1)S(1)}, bf16[32,4096]{1,0:T(8,128)(2,1)}, u32[]{:S(2)}) %copy-start) | copy-done | bytes 262168
  4.2 87.3 %shard_map.64 = bf16[6,4096]{1,0:T(8,128)(2,1)S(1)} custom-call(bf16[32,4096]{1,0:T(8,128)(2,1)S(1)} %copy-done, s32[2,256]{1,0:T(2,128)S(1)} %pad_add_fusion.meta_ref, f32[32,128]{1,0:T(8,128)S(1)} %broadcast_in_dim.6.info_ref, bf16[8,4096]{1,0:T(8,128)(2,1)S(1)} %pad.9.vec_ref, f32[5]{0:T(128)S(1)} %copy-done.1), custom_call_target="tpu_custom_call" | custom-call | tf_op jit(solution)/shard_map/pallas_call | solution.py:286
  91.4 0.6 copy.8
  (5 shorter events, 0.0 us)
Async XLA Ops:
  0.0 2.5 %copy-start.2 = (bf16[6,4096]{1,0:T(8,128)(2,1)S(1)}, bf16[6,4096]{1,0:T(8,128)(2,1)}, u32[]{:S(2)}) copy-start(bf16[6,4096]{1,0:T(8,128)(2,1)} %param.10) | copy-start | bytes 147460
  2.5 0.7 copy-start.1
  3.2 0.9 %copy-start = (bf16[32,4096]{1,0:T(8,128)(2,1)S(1)}, bf16[32,4096]{1,0:T(8,128)(2,1)}, u32[]{:S(2)}) copy-start(bf16[32,4096]{1,0:T(8,128)(2,1)} %tiles_ref.1) | copy-start | bytes 786436

commit v2 on v1

v2 whole, which is shorter than its diff:
```python
import jax
import jax.numpy as jnp
from jax import lax
from jax.experimental import pallas as pl
from jax.experimental.pallas import tpu as pltpu
from jax.sharding import PartitionSpec as P

TILE = 64
SLOTS_ROW = 16
REACH = 8
ITERS = 4
MESH = pl.DeviceIdType.MESH
F32 = jnp.float32
BF16 = jnp.bfloat16

N_ROWS = 24
N_TASK = 32
CHIPS = 384
CHIP_ROWS = 4
WINDOW = 5
OWN = 2
MINE = 6
PAD = 8
SOURCES = 16
HALF_VECTORS = MINE * SOURCES
GROUPS = 2
PART = HALF_VECTORS // GROUPS
PART_SOURCES = SOURCES // GROUPS
WIDTH = CHIP_ROWS * TILE


def turned(x, z):
    return x + (z & 1) * (3 - 2 * x)


def place(half, y, core):
    z = half >> 2
    x = turned(half & 3, z)
    upper = jnp.where(z >= 6, 1, 0)
    return (z - 6 * upper) * 4 + x, upper * 16 + y * 2 + core


def wrapped(index, size):
    index = jnp.where(index >= size, index - size, index)
    return jnp.where(index < 0, index + size, index)


def one_hot(condition):
    return jnp.where(condition, 1.0, 0.0).astype(BF16)


def iota(shape, dim):
    return lax.broadcasted_iota(jnp.int32, shape, dim)


def kernel(
    tiles_ref, target_ref, column_ref, count_ref, vec_ref, coef_ref, out_ref,
    tiles, send_h, recv_h, send_lab, recv_lab, send_info, recv_info, send_v, recv_v,
    band_raw, band, win, total, send_f, recv_f,
    h_send, lab_send, v_send, one_send, rim_send, f_send,
    load, h_recv, lab_recv, v_recv, info_recv, band_recv, rim_recv, f_recv,
):
    row, task = lax.axis_index("rows"), lax.axis_index("task")
    zh, y, core = task >> 4, (task >> 1) & 7, task & 1
    z, x = zh * 6 + (row >> 2), row & 3
    half = 4 * z + turned(x, z)
    chip = half * 8 + y

    def is_here(where):
        return (where[0] == row) & (where[1] == task)

    def transfer(src, dst, send_sem, recv_sem, where):
        here = is_here(where)

        @pl.when(here)
        def _():
            pltpu.make_async_copy(src, dst, recv_sem).start()

        @pl.when(jnp.logical_not(here))
        def _():
            pltpu.make_async_remote_copy(
                src, dst, send_sem, recv_sem, device_id=where, device_id_type=MESH
            ).start()

    def sent(src, send_sem, recv_sem, where):
        @pl.when(jnp.logical_not(is_here(where)))
        def _():
            pltpu.make_async_remote_copy(
                src, src, send_sem, recv_sem, device_id=where, device_id_type=MESH
            ).wait_send()

    def arrived(buffer, sem):
        pltpu.make_async_copy(buffer, buffer, sem).wait()

    def vector_owner(p):
        return place(2 * row + (p >> 3), p & 7, core)

    def vector_home(q):
        return half >> 1, (q >> 3) * 16 + (q & 7) * 2 + core

    def block_owner(to):
        return place(2 * to + zh, y, core)

    def rim_owner(away):
        other = wrapped(chip + away, CHIPS)
        return place(other >> 3, other & 7, core)

    load_tiles = pltpu.make_async_copy(tiles_ref, tiles, load)
    load_tiles.start()
    recv_lab[...] = jnp.zeros(recv_lab.shape, F32)

    barrier = pltpu.get_barrier_semaphore()

    def greet(where):
        @pl.when(jnp.logical_not(is_here(where)))
        def _():
            pl.semaphore_signal(barrier, inc=1, device_id=where, device_id_type=MESH)

    @pl.loop(0, SOURCES)
    def _(p):
        greet(vector_home(p))
        greet(vector_owner(p))

    @pl.loop(0, N_ROWS)
    def _(source):
        greet((source, (half & 1) * 16 + y * 2 + core))

    for away in (-2, 2, -1, 1):
        greet(rim_owner(away))
    greet((row, task + 1 - 2 * core))

    mine = vec_ref[...].astype(F32)
    for p in range(SOURCES):
        left = mine[:, p * WIDTH : p * WIDTH + 128]
        right = mine[:, p * WIDTH + 128 : (p + 1) * WIDTH]
        send_v[p] = jnp.concatenate([left, right], axis=0).astype(BF16)

    lane = iota((1, 32), 1)
    second_row = lane >> 4
    first = ((row * N_TASK + task) >> 1) * CHIP_ROWS - OWN * CHIP_ROWS
    live = (lane & 15) < jnp.where(second_row == 1, count_ref[0, 1], count_ref[0, 0])
    code = jnp.where(live, (column_ref[...] - first) * 2 + second_row + 1, 0)
    send_info[...] = jnp.zeros(send_info.shape, F32)
    send_info[0:1, 0:32] = code.astype(F32)

    target = target_ref[...]
    diagonal = iota((32, 32), 0) == iota((32, 32), 1)
    as_column = jnp.sum(jnp.where(diagonal, target, 0).astype(F32), axis=1, keepdims=True)
    as_column = as_column.astype(jnp.int32)
    owner_column, name_column = as_column >> 5, as_column & 31
    owner_row = target >> 5
    earlier = (owner_column == owner_row) & (iota((32, 32), 1) < iota((32, 32), 0))
    rank = jnp.sum(jnp.where(earlier, 1.0, 0.0), axis=1, keepdims=True)
    slot = (owner_column.astype(F32) * 2.0 + rank) * 8.0
    spread = (iota((32, 256), 1) & 31) == iota((32, 256), 0)
    slots = jnp.sum(jnp.where(spread, slot, 0.0), axis=0, keepdims=True)
    slots = slots.astype(jnp.int32) + (iota((1, 256), 1) >> 5)

    goes_to = one_hot(owner_row == (iota((N_ROWS * 8, 32), 0) >> 3))
    which = ((iota((32, 128), 1) >> 3) & 1).astype(F32) == rank
    named = jnp.where(which, (name_column + 1).astype(F32), 0.0).astype(BF16)
    names = jnp.dot(goes_to, named, preferred_element_type=F32) - 1.0
    send_lab[...] = names.reshape(N_ROWS, 8, 128)

    load_tiles.wait()
    stacked = jnp.concatenate([tiles[:, u * 512 : (u + 1) * 512] for u in range(8)], axis=0)
    packing = one_hot(iota((N_ROWS * 16, 256), 0) == slots)
    packed = jnp.dot(packing, stacked, preferred_element_type=F32)
    send_h[...] = packed.astype(BF16).reshape(N_ROWS, 16, 512)

    to_self = jnp.where((half & 1) == zh, 1, 0) + 2 * jnp.where((half >> 1) == row, 1, 0)
    pl.semaphore_wait(barrier, N_ROWS + 2 * SOURCES + 5 - to_self)

    slot_v = zh * 8 + y
    one_line = pl.ds(0, 1)
    info_owner = place(2 * row + zh, y, core)

    @pl.loop(0, SOURCES)
    def _(p):
        where = vector_owner(p)
        transfer(send_v.at[p], recv_v.at[slot_v], v_send.at[p], v_recv.at[zh], where)

    transfer(send_info.at[one_line], recv_info.at[one_line], one_send.at[0], info_recv, info_owner)

    @pl.loop(0, N_ROWS)
    def _(k):
        level = k >> 1
        far = 6 - ((level + 1) >> 1)
        there = wrapped(z + far * (2 * (level & 1) - 1), 12)
        to = 2 * there + (k & 1)
        where = block_owner(to)
        transfer(
            send_lab.at[to, one_line], recv_lab.at[row, one_line], lab_send.at[to], lab_recv, where
        )
        transfer(send_h.at[to], recv_h.at[row], h_send.at[to], h_recv, where)

    def selector(shape, vector_dim, side):
        where = iota(shape, 1 - vector_dim)
        at = where & 7
        vector = (where >> 4) * MINE + at
        fits = (at < MINE) & ((where & 8) == 8 * side)
        return one_hot((iota(shape, vector_dim) == vector) & fits)

    def rim(step, part, away):
        index = away + 2 if away < 0 else away + 1
        rows = pl.ds(part * PART, PART)
        return pltpu.make_async_remote_copy(
            win.at[step, OWN, rows],
            win.at[step, OWN - away, rows],
            rim_send.at[step, part, index],
            rim_recv.at[step, part, OWN - away],
            device_id=rim_owner(away),
            device_id_type=MESH,
        )

    def send_rims(step, part):
        for away in (-2, 2, -1, 1):
            rim(step, part, away).start()

    def rows_of(part):
        return slice(part * PART, (part + 1) * PART)

    for part in range(GROUPS):
        sources = pl.ds(part * PART_SOURCES, PART_SOURCES)
        arrived(recv_v.at[sources], v_recv.at[part])
        pieces = recv_v[sources].reshape(PART_SOURCES * 16, 128)
        for side in range(2):
            pick = selector((PART, PART_SOURCES * 16), 0, side)
            got = jnp.dot(pick, pieces, preferred_element_type=F32)
            win[0, OWN, rows_of(part), side * 128 : (side + 1) * 128] = got.astype(BF16)
        send_rims(0, part)
    total[...] = coef_ref[0] * win[0, OWN].astype(F32)

    arrived(recv_info.at[one_line], info_recv)
    arrived(recv_lab.at[:, one_line], lab_recv)
    wide = (N_ROWS * 8, N_ROWS * 16)
    lab = recv_lab[...].reshape(N_ROWS * 8, 128)
    lab = jnp.concatenate([lab] * 3, axis=1)
    keep = iota(wide, 0) == (iota(wide, 1) >> 4) * 8
    lab = jnp.sum(jnp.where(keep, lab, 0.0), axis=0, keepdims=True)
    on_diagonal = iota((32, 128), 0) == iota((32, 128), 1)
    info = jnp.sum(jnp.where(on_diagonal, recv_info[0:1, :], 0.0), axis=1, keepdims=True)
    at_slot = iota((32, N_ROWS * 16), 0).astype(F32) == lab
    code = jnp.sum(jnp.where(at_slot, info, 0.0), axis=0, keepdims=True) - 1.0
    goes = code * 8.0 + (iota((1, N_ROWS * 16), 1) & 7).astype(F32)
    columns = WINDOW * CHIP_ROWS
    placing = one_hot(iota((columns * 16, N_ROWS * 16), 0).astype(F32) == goes)
    at = iota((128, 128), 0)
    source = (at & 7) * 16 + (at >> 6) * 8 + ((at >> 3) & 7)
    turn = one_hot(iota((128, 128), 1) == source)

    arrived(recv_h, h_recv)
    blocks = recv_h[...].reshape(N_ROWS * 16, 512)
    raw = jnp.dot(placing, blocks, preferred_element_type=F32)
    low = iota((16, 128), 1) < TILE
    for pair_at in range(columns // 2):
        for group in range(4):
            lanes = slice(group * 128, (group + 1) * 128)
            a = raw[pair_at * 32 : pair_at * 32 + 16, lanes]
            b = raw[pair_at * 32 + 16 : pair_at * 32 + 32, lanes]
            even = jnp.where(low, a, pltpu.roll(b, TILE, 1))
            odd = jnp.where(low, pltpu.roll(a, TILE, 1), b)
            to = slice(pair_at * 128, (pair_at + 1) * 128)
            band_raw[group * 32 : group * 32 + 16, to] = even.astype(BF16)
            band_raw[group * 32 + 16 : group * 32 + 32, to] = odd.astype(BF16)
    mine_rows = pl.ds(pl.multiple_of(core * 128, 128), 128)
    band[mine_rows, :] = jnp.dot(turn, band_raw[...], preferred_element_type=F32).astype(BF16)
    sibling = pltpu.make_async_remote_copy(
        band.at[mine_rows],
        band.at[mine_rows],
        one_send.at[1],
        band_recv,
        device_id=(row, task + 1 - 2 * core),
        device_id_type=MESH,
    )
    sibling.start()
    sibling.wait_recv()

    slot_f = (half & 1) * 8 + y
    for step in range(ITERS):
        for part in range(GROUPS):
            rows = rows_of(part)
            product = None
            for j in (OWN, 1, 3, 0, 4):
                if j != OWN:
                    rim(step, part, OWN - j).wait_recv()
                term = lax.dot_general(
                    win[step, j, rows],
                    band[:, j * WIDTH : (j + 1) * WIDTH],
                    (((1,), (1,)), ((), ())),
                    preferred_element_type=F32,
                )
                product = term if product is None else product + term
            if step:
                product = 2.0 * product - win[step - 1, OWN, rows].astype(F32)
            current = product.astype(BF16)
            if step < ITERS - 1:
                win[step + 1, OWN, rows] = current
                send_rims(step + 1, part)
                total[rows] += coef_ref[step + 1] * current.astype(F32)
                continue
            result = (total[rows] + coef_ref[step + 1] * current.astype(F32)).astype(BF16)
            spread = None
            for side in range(2):
                put = selector((PART_SOURCES * 16, PART), 1, side)
                half_result = result[:, side * 128 : (side + 1) * 128]
                term = jnp.dot(put, half_result, preferred_element_type=F32)
                spread = term if spread is None else spread + term
            sources = slice(part * PART_SOURCES, (part + 1) * PART_SOURCES)
            send_f[sources] = spread.astype(BF16).reshape(PART_SOURCES, 16, 128)

            @pl.loop(part * PART_SOURCES, (part + 1) * PART_SOURCES)
            def _(q):
                where = vector_home(q)
                transfer(send_f.at[q], recv_f.at[slot_f], f_send.at[q], f_recv, where)

    @pl.loop(0, N_ROWS)
    def _(to):
        where = block_owner(to)
        sent(send_lab.at[to, one_line], lab_send.at[to], lab_recv, where)
        sent(send_h.at[to], h_send.at[to], h_recv, where)

    @pl.loop(0, SOURCES)
    def _(p):
        sent(send_v.at[p], v_send.at[p], v_recv.at[zh], vector_owner(p))
        sent(send_f.at[p], f_send.at[p], f_recv, vector_home(p))

    sent(send_info.at[one_line], one_send.at[0], info_recv, info_owner)
    sibling.wait_send()
    for step in range(ITERS):
        for part in range(GROUPS):
            for away in (-2, 2, -1, 1):
                rim(step, part, away).wait_send()

    arrived(recv_f, f_recv)
    final = recv_f[...].astype(F32)
    flat = [final[p, 8 * s : 8 * s + 8, :] for p in range(SOURCES) for s in range(2)]
    out_ref[...] = jnp.concatenate(flat, axis=1).astype(BF16)[:MINE, :]


def local(hamiltonian_tiles, tile_target, column_block, row_count, vectors, expansion_coef):
    padded = jnp.pad(vectors, ((0, PAD - MINE), (0, 0)))
    dma = pltpu.SemaphoreType.DMA
    vmem = pl.BlockSpec(memory_space=pltpu.VMEM)
    smem = pl.BlockSpec(memory_space=pltpu.SMEM)
    return pl.pallas_call(
        kernel,
        out_shape=jax.ShapeDtypeStruct(vectors.shape, BF16),
        in_specs=[pl.BlockSpec(memory_space=pl.ANY), vmem, vmem, smem, vmem, smem],
        out_specs=vmem,
        scratch_shapes=[
            pltpu.VMEM((32, TILE * TILE), BF16),
            pltpu.VMEM((N_ROWS, 16, 512), BF16),
            pltpu.VMEM((N_ROWS, 16, 512), BF16),
            pltpu.VMEM((N_ROWS, 8, 128), F32),
            pltpu.VMEM((N_ROWS, 8, 128), F32),
            pltpu.VMEM((8, 128), F32),
            pltpu.VMEM((8, 128), F32),
            pltpu.VMEM((SOURCES, 16, 128), BF16),
            pltpu.VMEM((SOURCES, 16, 128), BF16),
            pltpu.VMEM((128, WINDOW * WIDTH), BF16),
            pltpu.VMEM((WIDTH, WINDOW * WIDTH), BF16),
            pltpu.VMEM((ITERS, WINDOW, HALF_VECTORS, WIDTH), BF16),
            pltpu.VMEM((HALF_VECTORS, WIDTH), F32),
            pltpu.VMEM((SOURCES, 16, 128), BF16),
            pltpu.VMEM((SOURCES, 16, 128), BF16),
            dma((N_ROWS,)),
            dma((N_ROWS,)),
            dma((SOURCES,)),
            dma((2,)),
            dma((ITERS, GROUPS, 4)),
            dma((SOURCES,)),
            dma(()),
            dma(()),
            dma(()),
            dma((GROUPS,)),
            dma(()),
            dma(()),
            dma((ITERS, GROUPS, WINDOW)),
            dma(()),
        ],
        compiler_params=pltpu.CompilerParams(
            collective_id=0, has_side_effects=True, vmem_limit_bytes=32 * 1024 * 1024
        ),
    )(
        hamiltonian_tiles,
        tile_target[None, :],
        column_block[None, :],
        row_count[None, :],
        padded,
        expansion_coef,
    )


def solution(mesh):
    in_specs = (
        P(("rows", "task"), None),
        P(("rows", "task")),
        P(("rows", "task")),
        P(("rows", "task")),
        P("task", "rows"),
        P(),
    )
    out_specs = P("task", "rows")
    return jax.shard_map(local, mesh=mesh, in_specs=in_specs, out_specs=out_specs, check_vma=False)
```

time: 93.1 us -> 73.9 us (0.79)
  the two profiles are of different devices: /device:TPU:6 before, /device:TPU:130 now
where the time goes in v2:
time: 73.9 us; the launch traced here: 73.6 us
  Pallas kernels  71.1 us (96%)
  local copies, waits for them, and re-layouts  2.49 us (3%)
    pallas_call x1, Pallas kernels, local(): pl.pallas_call(kernel, out_shape=jax.ShapeDtypeStruct(vectors.shape, BF16...  71.1 us
    unnamed x11, local copies, waits for them, and re-layouts  1.59 us

profile of v2, /device:TPU:130, one launch (start us, length us, event | category | flops | bytes accessed | tf_op | source)
XLA Modules:
  0.0 73.6 jit_solution(1736088750083342768)
XLA Ops:
  0.0 0.0 copy-start.1
  0.0 0.0 copy-start.2
  0.0 0.0 copy-start.3
  0.0 0.0 copy-start.4
  0.0 0.9 %pad.4.vec_ref = bf16[8,4096]{1,0:T(8,128)(2,1)S(1)} pad(bf16[6,4096]{1,0:T(8,128)(2,1)} %param.10, bf16[]{:T(256)} %constant.2.clone.1), padding=0_2x0_0 | pad | bytes 114690 | tf_op jit(solution)/shard_map/jit(_pad)/pad | solution.py:342
  0.9 0.0 copy-done.1
  0.9 0.0 copy-done.2
  0.9 0.0 copy-done.3
  0.9 0.0 copy-done.4
  1.0 0.0 copy-start
  1.0 0.9 %copy-done = bf16[32,4096]{1,0:T(8,128)(2,1)S(1)} copy-done((bf16[32,4096]{1,0:T(8,128)(2,1)S(1)}, bf16[32,4096]{1,0:T(8,128)(2,1)}, u32[]{:S(2)}) %copy-start) | copy-done | bytes 262168
  1.9 71.1 %shard_map.64 = bf16[6,4096]{1,0:T(8,128)(2,1)S(1)} custom-call(bf16[32,4096]{1,0:T(8,128)(2,1)S(1)} %copy-done, s32[1,32]{1,0:T(1,128)S(1)} %bitcast.3, s32[1,32]{1,0:T(1,128)S(1)} %bitcast.4, s32[1,2]{1,0:T(1,128)S(1)} %bitcast.5, bf16[8,4096]{1,0:T(8,128)(2,1)S(1)} %pad.4.vec_ref, f32[5]{0:T(128)S(1)} %copy-done.4), custom_call_target="tpu_custom_call" | custom-call | tf_op jit(solution)/shard_map/pallas_call | solution.py:346
  73.0 0.6 copy.8
Async XLA Ops:
  0.0 0.9 %copy-start.1 = (s32[32]{0:T(128)S(1)}, s32[32]{0:T(128)}, u32[]{:S(2)}) copy-start(s32[32]{0:T(128)} %param.7) | copy-start | bytes 388
  0.0 0.9 %copy-start.2 = (s32[32]{0:T(128)S(1)}, s32[32]{0:T(128)}, u32[]{:S(2)}) copy-start(s32[32]{0:T(128)} %param.8) | copy-start | bytes 388
  0.0 0.9 %copy-start.3 = (s32[2]{0:T(128)S(1)}, s32[2]{0:T(128)}, u32[]{:S(2)}) copy-start(s32[2]{0:T(128)} %param.9) | copy-start | bytes 28
  0.0 0.9 %copy-start.4 = (f32[5]{0:T(128)S(1)}, f32[5]{0:T(128)}, u32[]{:S(2)}) copy-start(f32[5]{0:T(128)} %coef_ref.1) | copy-start | bytes 64
  1.0 1.0 %copy-start = (bf16[32,4096]{1,0:T(8,128)(2,1)S(1)}, bf16[32,4096]{1,0:T(8,128)(2,1)}, u32[]{:S(2)}) copy-start(bf16[32,4096]{1,0:T(8,128)(2,1)} %tiles_ref.1) | copy-start | bytes 786436

commit v3 on v2

--- a/solution.py
+++ b/solution.py
@@ -16,6 +16,7 @@
 N_ROWS = 24
 N_TASK = 32
 CHIPS = 384
+LEVELS = 12
 CHIP_ROWS = 4
 WINDOW = 5
 OWN = 2
@@ -23,9 +24,8 @@
 PAD = 8
 SOURCES = 16
 HALF_VECTORS = MINE * SOURCES
-GROUPS = 2
+GROUPS = 3
 PART = HALF_VECTORS // GROUPS
-PART_SOURCES = SOURCES // GROUPS
 WIDTH = CHIP_ROWS * TILE
 
 
@@ -33,11 +33,19 @@
     return x + (z & 1) * (3 - 2 * x)
 
 
-def place(half, y, core):
+def farthest_first(k, size):
+    return (size // 2 - ((k + 1) >> 1)) * (2 * (k & 1) - 1)
+
+
+def along(at, half):
+    return at + (half & 1) * (7 - 2 * at)
+
+
+def place(half, at, core):
     z = half >> 2
     x = turned(half & 3, z)
     upper = jnp.where(z >= 6, 1, 0)
-    return (z - 6 * upper) * 4 + x, upper * 16 + y * 2 + core
+    return (z - 6 * upper) * 4 + x, upper * 16 + along(at, half) * 2 + core
 
 
 def wrapped(index, size):
@@ -55,8 +63,8 @@
 
 def kernel(
     tiles_ref, target_ref, column_ref, count_ref, vec_ref, coef_ref, out_ref,
-    tiles, send_h, recv_h, send_lab, recv_lab, send_info, recv_info, send_v, recv_v,
-    band_raw, band, win, total, send_f, recv_f,
+    tiles, vec, padded, send_h, recv_h, send_lab, recv_lab, send_info, recv_info, send_v, recv_v,
+    band_raw, band, win, total, results, send_f, recv_f,
     h_send, lab_send, v_send, one_send, rim_send, f_send,
     load, h_recv, lab_recv, v_recv, info_recv, band_recv, rim_recv, f_recv,
 ):
@@ -64,7 +72,8 @@
     zh, y, core = task >> 4, (task >> 1) & 7, task & 1
     z, x = zh * 6 + (row >> 2), row & 3
     half = 4 * z + turned(x, z)
-    chip = half * 8 + y
+    at = along(y, half)
+    chip = half * 8 + at
 
     def is_here(where):
         return (where[0] == row) & (where[1] == task)
@@ -105,8 +114,10 @@
         other = wrapped(chip + away, CHIPS)
         return place(other >> 3, other & 7, core)
 
-    load_tiles = pltpu.make_async_copy(tiles_ref, tiles, load)
+    load_tiles = pltpu.make_async_copy(tiles_ref, tiles, load.at[0])
     load_tiles.start()
+    load_vec = pltpu.make_async_copy(vec_ref, vec, load.at[1])
+    load_vec.start()
     recv_lab[...] = jnp.zeros(recv_lab.shape, F32)
 
     barrier = pltpu.get_barrier_semaphore()
@@ -116,20 +127,23 @@
         def _():
             pl.semaphore_signal(barrier, inc=1, device_id=where, device_id_type=MESH)
 
+    @pl.loop(0, N_ROWS)
+    def _(source):
+        greet((source, (half & 1) * 16 + at * 2 + core))
+
     @pl.loop(0, SOURCES)
     def _(p):
         greet(vector_home(p))
         greet(vector_owner(p))
 
-    @pl.loop(0, N_ROWS)
-    def _(source):
-        greet((source, (half & 1) * 16 + y * 2 + core))
-
     for away in (-2, 2, -1, 1):
         greet(rim_owner(away))
     greet((row, task + 1 - 2 * core))
 
-    mine = vec_ref[...].astype(F32)
+    load_vec.wait()
+    padded[...] = jnp.zeros(padded.shape, F32)
+    padded[:MINE, :] = vec[...].astype(F32)
+    mine = padded[...]
     for p in range(SOURCES):
         left = mine[:, p * WIDTH : p * WIDTH + 128]
         right = mine[:, p * WIDTH + 128 : (p + 1) * WIDTH]
@@ -168,7 +182,7 @@
     packed = jnp.dot(packing, stacked, preferred_element_type=F32)
     send_h[...] = packed.astype(BF16).reshape(N_ROWS, 16, 512)
 
-    to_self = jnp.where((half & 1) == zh, 1, 0) + 2 * jnp.where((half >> 1) == row, 1, 0)
+    to_self = jnp.where(((half & 1) == zh) & (at == y), 1, 0) + 2 * jnp.where((half >> 1) == row, 1, 0)
     pl.semaphore_wait(barrier, N_ROWS + 2 * SOURCES + 5 - to_self)
 
     slot_v = zh * 8 + y
@@ -176,17 +190,15 @@
     info_owner = place(2 * row + zh, y, core)
 
     @pl.loop(0, SOURCES)
-    def _(p):
-        where = vector_owner(p)
-        transfer(send_v.at[p], recv_v.at[slot_v], v_send.at[p], v_recv.at[zh], where)
+    def _(k):
+        p = (k & 1) * 8 + ((y + farthest_first(k >> 1, 8)) & 7)
+        transfer(send_v.at[p], recv_v.at[slot_v], v_send.at[p], v_recv, vector_owner(p))
 
     transfer(send_info.at[one_line], recv_info.at[one_line], one_send.at[0], info_recv, info_owner)
 
     @pl.loop(0, N_ROWS)
     def _(k):
-        level = k >> 1
-        far = 6 - ((level + 1) >> 1)
-        there = wrapped(z + far * (2 * (level & 1) - 1), 12)
+        there = wrapped(z + farthest_first(k >> 1, LEVELS), LEVELS)
         to = 2 * there + (k & 1)
         where = block_owner(to)
         transfer(
@@ -194,11 +206,11 @@
         )
         transfer(send_h.at[to], recv_h.at[row], h_send.at[to], h_recv, where)
 
-    def selector(shape, vector_dim, side):
+    def selector(shape, vector_dim, side, source=0):
         where = iota(shape, 1 - vector_dim)
-        at = where & 7
-        vector = (where >> 4) * MINE + at
-        fits = (at < MINE) & ((where & 8) == 8 * side)
+        lane = where & 7
+        vector = ((where >> 4) + source) * MINE + lane
+        fits = (lane < MINE) & ((where & 8) == 8 * side)
         return one_hot((iota(shape, vector_dim) == vector) & fits)
 
     def rim(step, part, away):
@@ -220,14 +232,13 @@
     def rows_of(part):
         return slice(part * PART, (part + 1) * PART)
 
+    arrived(recv_v, v_recv)
+    pieces = recv_v[...].reshape(SOURCES * 16, 128)
+    for side in range(2):
+        pick = selector((HALF_VECTORS, SOURCES * 16), 0, side)
+        got = jnp.dot(pick, pieces, preferred_element_type=F32)
+        win[0, OWN, :, side * 128 : (side + 1) * 128] = got.astype(BF16)
     for part in range(GROUPS):
-        sources = pl.ds(part * PART_SOURCES, PART_SOURCES)
-        arrived(recv_v.at[sources], v_recv.at[part])
-        pieces = recv_v[sources].reshape(PART_SOURCES * 16, 128)
-        for side in range(2):
-            pick = selector((PART, PART_SOURCES * 16), 0, side)
-            got = jnp.dot(pick, pieces, preferred_element_type=F32)
-            win[0, OWN, rows_of(part), side * 128 : (side + 1) * 128] = got.astype(BF16)
         send_rims(0, part)
     total[...] = coef_ref[0] * win[0, OWN].astype(F32)
 
@@ -245,8 +256,8 @@
     goes = code * 8.0 + (iota((1, N_ROWS * 16), 1) & 7).astype(F32)
     columns = WINDOW * CHIP_ROWS
     placing = one_hot(iota((columns * 16, N_ROWS * 16), 0).astype(F32) == goes)
-    at = iota((128, 128), 0)
-    source = (at & 7) * 16 + (at >> 6) * 8 + ((at >> 3) & 7)
+    line = iota((128, 128), 0)
+    source = (line & 7) * 16 + (line >> 6) * 8 + ((line >> 3) & 7)
     turn = one_hot(iota((128, 128), 1) == source)
 
     arrived(recv_h, h_recv)
@@ -276,7 +287,7 @@
     sibling.start()
     sibling.wait_recv()
 
-    slot_f = (half & 1) * 8 + y
+    slot_f = (half & 1) * 8 + at
     for step in range(ITERS):
         for part in range(GROUPS):
             rows = rows_of(part)
@@ -299,17 +310,18 @@
                 send_rims(step + 1, part)
                 total[rows] += coef_ref[step + 1] * current.astype(F32)
                 continue
-            result = (total[rows] + coef_ref[step + 1] * current.astype(F32)).astype(BF16)
+            result = total[rows] + coef_ref[step + 1] * current.astype(F32)
+            results[rows, :] = result.astype(BF16)
+            begin, end = part * PART // MINE, (part + 1) * PART // MINE
             spread = None
             for side in range(2):
-                put = selector((PART_SOURCES * 16, PART), 1, side)
-                half_result = result[:, side * 128 : (side + 1) * 128]
-                term = jnp.dot(put, half_result, preferred_element_type=F32)
+                put = selector(((end - begin) * 16, (part + 1) * PART), 1, side, begin)
+                ready = results[: (part + 1) * PART, side * 128 : (side + 1) * 128]
+                term = jnp.dot(put, ready, preferred_element_type=F32)
                 spread = term if spread is None else spread + term
-            sources = slice(part * PART_SOURCES, (part + 1) * PART_SOURCES)
-            send_f[sources] = spread.astype(BF16).reshape(PART_SOURCES, 16, 128)
-
-            @pl.loop(part * PART_SOURCES, (part + 1) * PART_SOURCES)
+            send_f[begin:end] = spread.astype(BF16).reshape(end - begin, 16, 128)
+
+            @pl.loop(begin, end)
             def _(q):
                 where = vector_home(q)
                 transfer(send_f.at[q], recv_f.at[slot_f], f_send.at[q], f_recv, where)
@@ -322,7 +334,7 @@
 
     @pl.loop(0, SOURCES)
     def _(p):
-        sent(send_v.at[p], v_send.at[p], v_recv.at[zh], vector_owner(p))
+        sent(send_v.at[p], v_send.at[p], v_recv, vector_owner(p))
         sent(send_f.at[p], f_send.at[p], f_recv, vector_home(p))
 
     sent(send_info.at[one_line], one_send.at[0], info_recv, info_owner)
@@ -339,17 +351,19 @@
 
 
 def local(hamiltonian_tiles, tile_target, column_block, row_count, vectors, expansion_coef):
-    padded = jnp.pad(vectors, ((0, PAD - MINE), (0, 0)))
     dma = pltpu.SemaphoreType.DMA
     vmem = pl.BlockSpec(memory_space=pltpu.VMEM)
+    anywhere = pl.BlockSpec(memory_space=pl.ANY)
     smem = pl.BlockSpec(memory_space=pltpu.SMEM)
     return pl.pallas_call(
         kernel,
         out_shape=jax.ShapeDtypeStruct(vectors.shape, BF16),
-        in_specs=[pl.BlockSpec(memory_space=pl.ANY), vmem, vmem, smem, vmem, smem],
+        in_specs=[anywhere, vmem, vmem, smem, anywhere, smem],
         out_specs=vmem,
         scratch_shapes=[
             pltpu.VMEM((32, TILE * TILE), BF16),
+            pltpu.VMEM(vectors.shape, BF16),
+            pltpu.VMEM((PAD, vectors.shape[1]), F32),
             pltpu.VMEM((N_ROWS, 16, 512), BF16),
             pltpu.VMEM((N_ROWS, 16, 512), BF16),
             pltpu.VMEM((N_ROWS, 8, 128), F32),
@@ -362,6 +376,7 @@
             pltpu.VMEM((WIDTH, WINDOW * WIDTH), BF16),
             pltpu.VMEM((ITERS, WINDOW, HALF_VECTORS, WIDTH), BF16),
             pltpu.VMEM((HALF_VECTORS, WIDTH), F32),
+            pltpu.VMEM((HALF_VECTORS, WIDTH), BF16),
             pltpu.VMEM((SOURCES, 16, 128), BF16),
             pltpu.VMEM((SOURCES, 16, 128), BF16),
             dma((N_ROWS,)),
@@ -370,24 +385,24 @@
             dma((2,)),
             dma((ITERS, GROUPS, 4)),
             dma((SOURCES,)),
-            dma(()),
-            dma(()),
-            dma(()),
-            dma((GROUPS,)),
+            dma((2,)),
+            dma(()),
+            dma(()),
+            dma(()),
             dma(()),
             dma(()),
             dma((ITERS, GROUPS, WINDOW)),
             dma(()),
         ],
         compiler_params=pltpu.CompilerParams(
-            collective_id=0, has_side_effects=True, vmem_limit_bytes=32 * 1024 * 1024
+            collective_id=0, has_side_effects=True, vmem_limit_bytes=60 * 1024 * 1024
         ),
     )(
         hamiltonian_tiles,
         tile_target[None, :],
         column_block[None, :],
         row_count[None, :],
-        padded,
+        vectors,
         expansion_coef,
     )
 

time: 73.9 us -> 66.9 us (0.905)
  the two profiles are of different devices: /device:TPU:130 before, /device:TPU:6 now
where the time goes in v3:
time: 66.9 us; the launch traced here: 66.8 us
  Pallas kernels  65.3 us (98%)
  local copies, waits for them, and re-layouts  1.47 us (2%)
    pallas_call x1, Pallas kernels, local(): pl.pallas_call(kernel, out_shape=jax.ShapeDtypeStruct(vectors.shape, BF16...  65.3 us
    unnamed x1, local copies, waits for them, and re-layouts  1.47 us

profile of v3, /device:TPU:6, one launch (start us, length us, event | category | flops | bytes accessed | tf_op | source)
XLA Modules:
  0.0 66.8 jit_solution(1938809770552371264)
XLA Ops:
  0.0 65.3 %shard_map.64 = bf16[6,4096]{1,0:T(8,128)(2,1)} custom-call(bf16[32,4096]{1,0:T(8,128)(2,1)} %tiles_ref.1, s32[1,32]{1,0:T(1,128)} %bitcast.3, s32[1,32]{1,0:T(1,128)} %bitcast.4, s32[1,2]{1,0:T(1,128)} %bitcast.5, bf16[6,4096]{1,0:T(8,128)(2,1)} %vec_ref.1, f32[5]{0:T(128)} %coef_ref.1), custom_call_target="tpu_custom_call" | custom-call | tf_op jit(solution)/shard_map/pallas_call | solution.py:358
  65.3 1.5 %copy.8 = bf16[6,4096]{1,0:T(8,128)(2,1)} copy(bf16[6,4096]{1,0:T(8,128)(2,1)} %shard_map.64) | data formatting | bytes 98304

commit v4 on v3

--- a/solution.py
+++ b/solution.py
@@ -63,7 +63,7 @@
 
 def kernel(
     tiles_ref, target_ref, column_ref, count_ref, vec_ref, coef_ref, out_ref,
-    tiles, vec, padded, send_h, recv_h, send_lab, recv_lab, send_info, recv_info, send_v, recv_v,
+    tiles, target, column, count, vec, coef, padded, send_h, recv_h, send_lab, recv_lab, send_info, recv_info, send_v, recv_v,
     band_raw, band, win, total, results, send_f, recv_f,
     h_send, lab_send, v_send, one_send, rim_send, f_send,
     load, h_recv, lab_recv, v_recv, info_recv, band_recv, rim_recv, f_recv,
@@ -91,15 +91,17 @@
                 src, dst, send_sem, recv_sem, device_id=where, device_id_type=MESH
             ).start()
 
-    def sent(src, send_sem, recv_sem, where):
-        @pl.when(jnp.logical_not(is_here(where)))
-        def _():
-            pltpu.make_async_remote_copy(
-                src, src, send_sem, recv_sem, device_id=where, device_id_type=MESH
-            ).wait_send()
-
     def arrived(buffer, sem):
         pltpu.make_async_copy(buffer, buffer, sem).wait()
+
+    def sent(buffer, sem, one_stays):
+        @pl.when(one_stays)
+        def _():
+            arrived(buffer.at[pl.ds(1, buffer.shape[0] - 1)], sem)
+
+        @pl.when(jnp.logical_not(one_stays))
+        def _():
+            arrived(buffer, sem)
 
     def vector_owner(p):
         return place(2 * row + (p >> 3), p & 7, core)
@@ -114,10 +116,21 @@
         other = wrapped(chip + away, CHIPS)
         return place(other >> 3, other & 7, core)
 
-    load_tiles = pltpu.make_async_copy(tiles_ref, tiles, load.at[0])
-    load_tiles.start()
-    load_vec = pltpu.make_async_copy(vec_ref, vec, load.at[1])
-    load_vec.start()
+    loads = [
+        pltpu.make_async_copy(src, dst, load.at[i])
+        for i, (src, dst) in enumerate(
+            (
+                (target_ref, target),
+                (column_ref, column),
+                (count_ref, count),
+                (coef_ref, coef),
+                (vec_ref, vec),
+                (tiles_ref, tiles),
+            )
+        )
+    ]
+    for copy in loads:
+        copy.start()
     recv_lab[...] = jnp.zeros(recv_lab.shape, F32)
 
     barrier = pltpu.get_barrier_semaphore()
@@ -140,7 +153,8 @@
         greet(rim_owner(away))
     greet((row, task + 1 - 2 * core))
 
-    load_vec.wait()
+    for copy in loads[:-1]:
+        copy.wait()
     padded[...] = jnp.zeros(padded.shape, F32)
     padded[:MINE, :] = vec[...].astype(F32)
     mine = padded[...]
@@ -152,17 +166,17 @@
     lane = iota((1, 32), 1)
     second_row = lane >> 4
     first = ((row * N_TASK + task) >> 1) * CHIP_ROWS - OWN * CHIP_ROWS
-    live = (lane & 15) < jnp.where(second_row == 1, count_ref[0, 1], count_ref[0, 0])
-    code = jnp.where(live, (column_ref[...] - first) * 2 + second_row + 1, 0)
+    live = (lane & 15) < jnp.where(second_row == 1, count[:, 1:2], count[:, 0:1])
+    code = jnp.where(live, (column[...] - first) * 2 + second_row + 1, 0)
     send_info[...] = jnp.zeros(send_info.shape, F32)
     send_info[0:1, 0:32] = code.astype(F32)
 
-    target = target_ref[...]
+    targets = target[...]
     diagonal = iota((32, 32), 0) == iota((32, 32), 1)
-    as_column = jnp.sum(jnp.where(diagonal, target, 0).astype(F32), axis=1, keepdims=True)
+    as_column = jnp.sum(jnp.where(diagonal, targets, 0).astype(F32), axis=1, keepdims=True)
     as_column = as_column.astype(jnp.int32)
     owner_column, name_column = as_column >> 5, as_column & 31
-    owner_row = target >> 5
+    owner_row = targets >> 5
     earlier = (owner_column == owner_row) & (iota((32, 32), 1) < iota((32, 32), 0))
     rank = jnp.sum(jnp.where(earlier, 1.0, 0.0), axis=1, keepdims=True)
     slot = (owner_column.astype(F32) * 2.0 + rank) * 8.0
@@ -176,13 +190,15 @@
     names = jnp.dot(goes_to, named, preferred_element_type=F32) - 1.0
     send_lab[...] = names.reshape(N_ROWS, 8, 128)
 
-    load_tiles.wait()
+    loads[-1].wait()
     stacked = jnp.concatenate([tiles[:, u * 512 : (u + 1) * 512] for u in range(8)], axis=0)
     packing = one_hot(iota((N_ROWS * 16, 256), 0) == slots)
     packed = jnp.dot(packing, stacked, preferred_element_type=F32)
     send_h[...] = packed.astype(BF16).reshape(N_ROWS, 16, 512)
 
-    to_self = jnp.where(((half & 1) == zh) & (at == y), 1, 0) + 2 * jnp.where((half >> 1) == row, 1, 0)
+    block_stays = ((half & 1) == zh) & (at == y)
+    vector_stays = (half >> 1) == row
+    to_self = jnp.where(block_stays, 1, 0) + 2 * jnp.where(vector_stays, 1, 0)
     pl.semaphore_wait(barrier, N_ROWS + 2 * SOURCES + 5 - to_self)
 
     slot_v = zh * 8 + y
@@ -192,7 +208,7 @@
     @pl.loop(0, SOURCES)
     def _(k):
         p = (k & 1) * 8 + ((y + farthest_first(k >> 1, 8)) & 7)
-        transfer(send_v.at[p], recv_v.at[slot_v], v_send.at[p], v_recv, vector_owner(p))
+        transfer(send_v.at[p], recv_v.at[slot_v], v_send, v_recv, vector_owner(p))
 
     transfer(send_info.at[one_line], recv_info.at[one_line], one_send.at[0], info_recv, info_owner)
 
@@ -202,9 +218,9 @@
         to = 2 * there + (k & 1)
         where = block_owner(to)
         transfer(
-            send_lab.at[to, one_line], recv_lab.at[row, one_line], lab_send.at[to], lab_recv, where
+            send_lab.at[to, one_line], recv_lab.at[row, one_line], lab_send, lab_recv, where
         )
-        transfer(send_h.at[to], recv_h.at[row], h_send.at[to], h_recv, where)
+        transfer(send_h.at[to], recv_h.at[row], h_send, h_recv, where)
 
     def selector(shape, vector_dim, side, source=0):
         where = iota(shape, 1 - vector_dim)
@@ -214,12 +230,11 @@
         return one_hot((iota(shape, vector_dim) == vector) & fits)
 
     def rim(step, part, away):
-        index = away + 2 if away < 0 else away + 1
         rows = pl.ds(part * PART, PART)
         return pltpu.make_async_remote_copy(
             win.at[step, OWN, rows],
             win.at[step, OWN - away, rows],
-            rim_send.at[step, part, index],
+            rim_send.at[step],
             rim_recv.at[step, part, OWN - away],
             device_id=rim_owner(away),
             device_id_type=MESH,
@@ -228,6 +243,9 @@
     def send_rims(step, part):
         for away in (-2, 2, -1, 1):
             rim(step, part, away).start()
+
+    def rims_sent(step):
+        arrived(win.at[step, pl.ds(0, 4)], rim_send.at[step])
 
     def rows_of(part):
         return slice(part * PART, (part + 1) * PART)
@@ -240,7 +258,7 @@
         win[0, OWN, :, side * 128 : (side + 1) * 128] = got.astype(BF16)
     for part in range(GROUPS):
         send_rims(0, part)
-    total[...] = coef_ref[0] * win[0, OWN].astype(F32)
+    total[...] = coef[:, 0:1] * win[0, OWN].astype(F32)
 
     arrived(recv_info.at[one_line], info_recv)
     arrived(recv_lab.at[:, one_line], lab_recv)
@@ -287,6 +305,21 @@
     sibling.start()
     sibling.wait_recv()
 
+    def leave(step):
+        if step == 0:
+            sent(send_h, h_send, block_stays)
+            sent(send_lab.at[:, one_line], lab_send, block_stays)
+        elif step == 1:
+            sent(send_v, v_send, vector_stays)
+            sibling.wait_send()
+
+            @pl.when(jnp.logical_not(block_stays & vector_stays))
+            def _():
+                arrived(send_info.at[one_line], one_send.at[0])
+
+        if 1 <= step < ITERS:
+            rims_sent(step - 1)
+
     slot_f = (half & 1) * 8 + at
     for step in range(ITERS):
         for part in range(GROUPS):
@@ -308,9 +341,11 @@
             if step < ITERS - 1:
                 win[step + 1, OWN, rows] = current
                 send_rims(step + 1, part)
-                total[rows] += coef_ref[step + 1] * current.astype(F32)
+                total[rows] += coef[:, step + 1 : step + 2] * current.astype(F32)
+                if part == GROUPS - 1:
+                    leave(step)
                 continue
-            result = total[rows] + coef_ref[step + 1] * current.astype(F32)
+            result = total[rows] + coef[:, step + 1 : step + 2] * current.astype(F32)
             results[rows, :] = result.astype(BF16)
             begin, end = part * PART // MINE, (part + 1) * PART // MINE
             spread = None
@@ -324,26 +359,11 @@
             @pl.loop(begin, end)
             def _(q):
                 where = vector_home(q)
-                transfer(send_f.at[q], recv_f.at[slot_f], f_send.at[q], f_recv, where)
-
-    @pl.loop(0, N_ROWS)
-    def _(to):
-        where = block_owner(to)
-        sent(send_lab.at[to, one_line], lab_send.at[to], lab_recv, where)
-        sent(send_h.at[to], h_send.at[to], h_recv, where)
-
-    @pl.loop(0, SOURCES)
-    def _(p):
-        sent(send_v.at[p], v_send.at[p], v_recv, vector_owner(p))
-        sent(send_f.at[p], f_send.at[p], f_recv, vector_home(p))
-
-    sent(send_info.at[one_line], one_send.at[0], info_recv, info_owner)
-    sibling.wait_send()
-    for step in range(ITERS):
-        for part in range(GROUPS):
-            for away in (-2, 2, -1, 1):
-                rim(step, part, away).wait_send()
-
+                transfer(send_f.at[q], recv_f.at[slot_f], f_send, f_recv, where)
+
+    leave(ITERS - 1)
+    rims_sent(ITERS - 1)
+    sent(send_f, f_send, vector_stays)
     arrived(recv_f, f_recv)
     final = recv_f[...].astype(F32)
     flat = [final[p, 8 * s : 8 * s + 8, :] for p in range(SOURCES) for s in range(2)]
@@ -354,15 +374,18 @@
     dma = pltpu.SemaphoreType.DMA
     vmem = pl.BlockSpec(memory_space=pltpu.VMEM)
     anywhere = pl.BlockSpec(memory_space=pl.ANY)
-    smem = pl.BlockSpec(memory_space=pltpu.SMEM)
     return pl.pallas_call(
         kernel,
         out_shape=jax.ShapeDtypeStruct(vectors.shape, BF16),
-        in_specs=[anywhere, vmem, vmem, smem, anywhere, smem],
+        in_specs=[anywhere] * 6,
         out_specs=vmem,
         scratch_shapes=[
             pltpu.VMEM((32, TILE * TILE), BF16),
+            pltpu.VMEM((1, 32), jnp.int32),
+            pltpu.VMEM((1, 32), jnp.int32),
+            pltpu.VMEM((1, 2), jnp.int32),
             pltpu.VMEM(vectors.shape, BF16),
+            pltpu.VMEM((1, ITERS + 1), F32),
             pltpu.VMEM((PAD, vectors.shape[1]), F32),
             pltpu.VMEM((N_ROWS, 16, 512), BF16),
             pltpu.VMEM((N_ROWS, 16, 512), BF16),
@@ -379,13 +402,13 @@
             pltpu.VMEM((HALF_VECTORS, WIDTH), BF16),
             pltpu.VMEM((SOURCES, 16, 128), BF16),
             pltpu.VMEM((SOURCES, 16, 128), BF16),
-            dma((N_ROWS,)),
-            dma((N_ROWS,)),
-            dma((SOURCES,)),
+            dma(()),
+            dma(()),
+            dma(()),
             dma((2,)),
-            dma((ITERS, GROUPS, 4)),
-            dma((SOURCES,)),
-            dma((2,)),
+            dma((ITERS,)),
+            dma(()),
+            dma((6,)),
             dma(()),
             dma(()),
             dma(()),
@@ -395,7 +418,7 @@
             dma(()),
         ],
         compiler_params=pltpu.CompilerParams(
-            collective_id=0, has_side_effects=True, vmem_limit_bytes=60 * 1024 * 1024
+            collective_id=0, has_side_effects=True, vmem_limit_bytes=55104 * 1024
         ),
     )(
         hamiltonian_tiles,
@@ -403,7 +426,7 @@
         column_block[None, :],
         row_count[None, :],
         vectors,
-        expansion_coef,
+        expansion_coef[None, :],
     )
 
 

time: 66.9 us -> 64.3 us (0.961)
  Pallas kernels: 65.3 us -> 62.6 us
    pallas_call x1, Pallas kernels: 65.3 us -> 62.6 us  [local(): pl.pallas_call(kernel, out_shape=jax.ShapeDtypeStruct(vectors.shape, BF16...]
    unnamed x1 -> x9, local copies, waits for them, and re-layouts: 1.47 us -> 1.32 us
where the time goes in v4:
time: 64.3 us; the launch traced here: 63.9 us
  Pallas kernels  62.6 us (97%)
  local copies, waits for them, and re-layouts  1.32 us (2%)
    pallas_call x1, Pallas kernels, local(): pl.pallas_call(kernel, out_shape=jax.ShapeDtypeStruct(vectors.shape, BF16...  62.6 us
    unnamed x9, local copies, waits for them, and re-layouts  1.32 us

profile of v4, /device:TPU:6, one launch (start us, length us, event | category | flops | bytes accessed | tf_op | source)
XLA Modules:
  0.0 63.9 jit_solution(8064998076812710752)
XLA Ops:
  0.0 0.0 copy-start.3
  0.0 0.0 copy-start
  0.0 0.0 copy-start.1
  0.0 0.0 copy-start.2
  0.0 0.6 copy-done.3
  0.7 0.0 copy-done
  0.7 0.0 copy-done.1
  0.7 0.0 copy-done.2
  0.7 62.6 %shard_map.64 = bf16[6,4096]{1,0:T(8,128)(2,1)S(1)} custom-call(bf16[32,4096]{1,0:T(8,128)(2,1)} %tiles_ref.1, s32[1,32]{1,0:T(1,128)S(1)} %bitcast.4, s32[1,32]{1,0:T(1,128)S(1)} %bitcast.5, s32[1,2]{1,0:T(1,128)S(1)} %bitcast.6, bf16[6,4096]{1,0:T(8,128)(2,1)} %vec_ref.1, f32[1,5]{1,0:T(1,128)S(1)} %bitcast.7), custom_call_target="tpu_custom_call" | custom-call | tf_op jit(solution)/shard_map/pallas_call | solution.py:377
  63.3 0.6 copy.8
Async XLA Ops:
  0.0 0.7 %copy-start.3 = (f32[5]{0:T(128)S(1)}, f32[5]{0:T(128)}, u32[]{:S(2)}) copy-start(f32[5]{0:T(128)} %param.11) | copy-start | bytes 64
  0.0 0.7 %copy-start = (s32[32]{0:T(128)S(1)}, s32[32]{0:T(128)}, u32[]{:S(2)}) copy-start(s32[32]{0:T(128)} %param.7) | copy-start | bytes 388
  0.0 0.7 %copy-start.1 = (s32[32]{0:T(128)S(1)}, s32[32]{0:T(128)}, u32[]{:S(2)}) copy-start(s32[32]{0:T(128)} %param.8) | copy-start | bytes 388
  0.0 0.7 %copy-start.2 = (s32[2]{0:T(128)S(1)}, s32[2]{0:T(128)}, u32[]{:S(2)}) copy-start(s32[2]{0:T(128)} %param.9) | copy-start | bytes 28

commit v5 on v4

--- a/solution.py
+++ b/solution.py
@@ -24,7 +24,7 @@
 PAD = 8
 SOURCES = 16
 HALF_VECTORS = MINE * SOURCES
-GROUPS = 3
+GROUPS = 6
 PART = HALF_VECTORS // GROUPS
 WIDTH = CHIP_ROWS * TILE
 
@@ -64,7 +64,7 @@
 def kernel(
     tiles_ref, target_ref, column_ref, count_ref, vec_ref, coef_ref, out_ref,
     tiles, target, column, count, vec, coef, padded, send_h, recv_h, send_lab, recv_lab, send_info, recv_info, send_v, recv_v,
-    band_raw, band, win, total, results, send_f, recv_f,
+    band_raw, band, band_t, win, total, results, send_f, recv_f,
     h_send, lab_send, v_send, one_send, rim_send, f_send,
     load, h_recv, lab_recv, v_recv, info_recv, band_recv, rim_recv, f_recv,
 ):
@@ -78,6 +78,11 @@
     def is_here(where):
         return (where[0] == row) & (where[1] == task)
 
+    def send(src, dst, send_sem, recv_sem, where):
+        pltpu.make_async_remote_copy(
+            src, dst, send_sem, recv_sem, device_id=where, device_id_type=MESH
+        ).start()
+
     def transfer(src, dst, send_sem, recv_sem, where):
         here = is_here(where)
 
@@ -87,9 +92,7 @@
 
         @pl.when(jnp.logical_not(here))
         def _():
-            pltpu.make_async_remote_copy(
-                src, dst, send_sem, recv_sem, device_id=where, device_id_type=MESH
-            ).start()
+            send(src, dst, send_sem, recv_sem, where)
 
     def arrived(buffer, sem):
         pltpu.make_async_copy(buffer, buffer, sem).wait()
@@ -136,18 +139,32 @@
     barrier = pltpu.get_barrier_semaphore()
 
     def greet(where):
-        @pl.when(jnp.logical_not(is_here(where)))
-        def _():
-            pl.semaphore_signal(barrier, inc=1, device_id=where, device_id_type=MESH)
-
-    @pl.loop(0, N_ROWS)
-    def _(source):
-        greet((source, (half & 1) * 16 + at * 2 + core))
-
-    @pl.loop(0, SOURCES)
-    def _(p):
-        greet(vector_home(p))
-        greet(vector_owner(p))
+        pl.semaphore_signal(barrier, inc=1, device_id=where, device_id_type=MESH)
+
+    block_stays = ((half & 1) == zh) & (at == y)
+    vector_stays = (half >> 1) == row
+    slot_v, slot_f = zh * 8 + y, (half & 1) * 8 + at
+
+    def block_home(source):
+        return source, (half & 1) * 16 + at * 2 + core
+
+    @pl.loop(1, N_ROWS)
+    def _(k):
+        greet(block_home(wrapped(row + k, N_ROWS)))
+
+    @pl.loop(1, SOURCES)
+    def _(k):
+        greet(vector_home((slot_v + k) & 15))
+        greet(vector_owner((slot_f + k) & 15))
+
+    @pl.when(jnp.logical_not(block_stays))
+    def _():
+        greet(block_home(row))
+
+    @pl.when(jnp.logical_not(vector_stays))
+    def _():
+        greet(vector_home(slot_v))
+        greet(vector_owner(slot_f))
 
     for away in (-2, 2, -1, 1):
         greet(rim_owner(away))
@@ -196,31 +213,38 @@
     packed = jnp.dot(packing, stacked, preferred_element_type=F32)
     send_h[...] = packed.astype(BF16).reshape(N_ROWS, 16, 512)
 
-    block_stays = ((half & 1) == zh) & (at == y)
-    vector_stays = (half >> 1) == row
     to_self = jnp.where(block_stays, 1, 0) + 2 * jnp.where(vector_stays, 1, 0)
     pl.semaphore_wait(barrier, N_ROWS + 2 * SOURCES + 5 - to_self)
 
-    slot_v = zh * 8 + y
     one_line = pl.ds(0, 1)
     info_owner = place(2 * row + zh, y, core)
 
-    @pl.loop(0, SOURCES)
+    def send_vectors(k, move):
+        p = (slot_f + k) & 15
+        move(send_v.at[p], recv_v.at[slot_v], v_send, v_recv, vector_owner(p))
+
+    @pl.loop(1, SOURCES)
     def _(k):
-        p = (k & 1) * 8 + ((y + farthest_first(k >> 1, 8)) & 7)
-        transfer(send_v.at[p], recv_v.at[slot_v], v_send, v_recv, vector_owner(p))
+        send_vectors(k, send)
+
+    send_vectors(0, transfer)
 
     transfer(send_info.at[one_line], recv_info.at[one_line], one_send.at[0], info_recv, info_owner)
 
-    @pl.loop(0, N_ROWS)
-    def _(k):
+    def send_blocks(k, move):
         there = wrapped(z + farthest_first(k >> 1, LEVELS), LEVELS)
         to = 2 * there + (k & 1)
         where = block_owner(to)
-        transfer(
-            send_lab.at[to, one_line], recv_lab.at[row, one_line], lab_send, lab_recv, where
-        )
-        transfer(send_h.at[to], recv_h.at[row], h_send, h_recv, where)
+        lab = send_lab.at[to, one_line], recv_lab.at[row, one_line]
+        move(*lab, lab_send, lab_recv, where)
+        move(send_h.at[to], recv_h.at[row], h_send, h_recv, where)
+
+    @pl.loop(0, N_ROWS - 2)
+    def _(k):
+        send_blocks(k, send)
+
+    for k in (N_ROWS - 2, N_ROWS - 1):
+        send_blocks(k, transfer)
 
     def selector(shape, vector_dim, side, source=0):
         where = iota(shape, 1 - vector_dim)
@@ -304,6 +328,7 @@
     )
     sibling.start()
     sibling.wait_recv()
+    band_t[...] = band[...].T
 
     def leave(step):
         if step == 0:
@@ -320,7 +345,6 @@
         if 1 <= step < ITERS:
             rims_sent(step - 1)
 
-    slot_f = (half & 1) * 8 + at
     for step in range(ITERS):
         for part in range(GROUPS):
             rows = rows_of(part)
@@ -330,8 +354,8 @@
                     rim(step, part, OWN - j).wait_recv()
                 term = lax.dot_general(
                     win[step, j, rows],
-                    band[:, j * WIDTH : (j + 1) * WIDTH],
-                    (((1,), (1,)), ((), ())),
+                    band_t[j * WIDTH : (j + 1) * WIDTH, :],
+                    (((1,), (0,)), ((), ())),
                     preferred_element_type=F32,
                 )
                 product = term if product is None else product + term
@@ -397,6 +421,7 @@
             pltpu.VMEM((SOURCES, 16, 128), BF16),
             pltpu.VMEM((128, WINDOW * WIDTH), BF16),
             pltpu.VMEM((WIDTH, WINDOW * WIDTH), BF16),
+            pltpu.VMEM((WINDOW * WIDTH, WIDTH), BF16),
             pltpu.VMEM((ITERS, WINDOW, HALF_VECTORS, WIDTH), BF16),
             pltpu.VMEM((HALF_VECTORS, WIDTH), F32),
             pltpu.VMEM((HALF_VECTORS, WIDTH), BF16),

time: 64.3 us -> 63.4 us (0.986)
  no operation moved by 1% of the time
where the time goes in v5:
time: 63.4 us; the launch traced here: 63.3 us
  Pallas kernels  62 us (98%)
  local copies, waits for them, and re-layouts  1.32 us (2%)
    pallas_call x1, Pallas kernels, local(): pl.pallas_call(kernel, out_shape=jax.ShapeDtypeStruct(vectors.shape, BF16...  62 us
    unnamed x9, local copies, waits for them, and re-layouts  1.32 us

profile of v5, /device:TPU:6, one launch (start us, length us, event | category | flops | bytes accessed | tf_op | source)
XLA Modules:
  0.0 63.3 jit_solution(2395649457639692671)
XLA Ops:
  0.0 0.0 copy-start.3
  0.0 0.0 copy-start
  0.0 0.0 copy-start.1
  0.0 0.0 copy-start.2
  0.0 0.6 %copy-done.3 = f32[5]{0:T(128)S(1)} copy-done((f32[5]{0:T(128)S(1)}, f32[5]{0:T(128)}, u32[]{:S(2)}) %copy-start.3) | copy-done | bytes 44
  0.7 0.0 copy-done
  0.7 0.0 copy-done.1
  0.7 0.0 copy-done.2
  0.7 62.0 %shard_map.64 = bf16[6,4096]{1,0:T(8,128)(2,1)S(1)} custom-call(bf16[32,4096]{1,0:T(8,128)(2,1)} %tiles_ref.1, s32[1,32]{1,0:T(1,128)S(1)} %bitcast.4, s32[1,32]{1,0:T(1,128)S(1)} %bitcast.5, s32[1,2]{1,0:T(1,128)S(1)} %bitcast.6, bf16[6,4096]{1,0:T(8,128)(2,1)} %vec_ref.1, f32[1,5]{1,0:T(1,128)S(1)} %bitcast.7), custom_call_target="tpu_custom_call" | custom-call | tf_op jit(solution)/shard_map/pallas_call | solution.py:401
  62.7 0.6 copy.8
Async XLA Ops:
  0.0 0.7 %copy-start.3 = (f32[5]{0:T(128)S(1)}, f32[5]{0:T(128)}, u32[]{:S(2)}) copy-start(f32[5]{0:T(128)} %param.11) | copy-start | bytes 64
  0.0 0.7 %copy-start = (s32[32]{0:T(128)S(1)}, s32[32]{0:T(128)}, u32[]{:S(2)}) copy-start(s32[32]{0:T(128)} %param.7) | copy-start | bytes 388
  0.0 0.7 %copy-start.1 = (s32[32]{0:T(128)S(1)}, s32[32]{0:T(128)}, u32[]{:S(2)}) copy-start(s32[32]{0:T(128)} %param.8) | copy-start | bytes 388
  0.0 0.7 %copy-start.2 = (s32[2]{0:T(128)S(1)}, s32[2]{0:T(128)}, u32[]{:S(2)}) copy-start(s32[2]{0:T(128)} %param.9) | copy-start | bytes 28

commit v6 on v5

--- a/solution.py
+++ b/solution.py
@@ -27,6 +27,7 @@
 GROUPS = 6
 PART = HALF_VECTORS // GROUPS
 WIDTH = CHIP_ROWS * TILE
+HALF_BAND = WINDOW * WIDTH // 2
 
 
 def turned(x, z):
@@ -317,18 +318,27 @@
             band_raw[group * 32 : group * 32 + 16, to] = even.astype(BF16)
             band_raw[group * 32 + 16 : group * 32 + 32, to] = odd.astype(BF16)
     mine_rows = pl.ds(pl.multiple_of(core * 128, 128), 128)
-    band[mine_rows, :] = jnp.dot(turn, band_raw[...], preferred_element_type=F32).astype(BF16)
-    sibling = pltpu.make_async_remote_copy(
-        band.at[mine_rows],
-        band.at[mine_rows],
-        one_send.at[1],
-        band_recv,
-        device_id=(row, task + 1 - 2 * core),
-        device_id_type=MESH,
-    )
-    sibling.start()
-    sibling.wait_recv()
-    band_t[...] = band[...].T
+    siblings = []
+    for piece in range(2):
+        columns = slice(piece * HALF_BAND, (piece + 1) * HALF_BAND)
+        turned_rows = jnp.dot(turn, band_raw[:, columns], preferred_element_type=F32)
+        band[mine_rows, columns] = turned_rows.astype(BF16)
+        copy = pltpu.make_async_remote_copy(
+            band.at[mine_rows, columns],
+            band.at[mine_rows, columns],
+            one_send.at[1 + piece],
+            band_recv.at[piece],
+            device_id=(row, task + 1 - 2 * core),
+            device_id_type=MESH,
+        )
+        copy.start()
+        siblings.append(copy)
+    their_rows = pl.ds(pl.multiple_of((1 - core) * 128, 128), 128)
+    band_t[:, mine_rows] = band[mine_rows, :].T
+    for piece in range(2):
+        columns = slice(piece * HALF_BAND, (piece + 1) * HALF_BAND)
+        siblings[piece].wait_recv()
+        band_t[columns, their_rows] = band[their_rows, columns].T
 
     def leave(step):
         if step == 0:
@@ -336,7 +346,8 @@
             sent(send_lab.at[:, one_line], lab_send, block_stays)
         elif step == 1:
             sent(send_v, v_send, vector_stays)
-            sibling.wait_send()
+            for copy in siblings:
+                copy.wait_send()
 
             @pl.when(jnp.logical_not(block_stays & vector_stays))
             def _():
@@ -430,15 +441,15 @@
             dma(()),
             dma(()),
             dma(()),
+            dma((3,)),
+            dma((ITERS,)),
+            dma(()),
+            dma((6,)),
+            dma(()),
+            dma(()),
+            dma(()),
+            dma(()),
             dma((2,)),
-            dma((ITERS,)),
-            dma(()),
-            dma((6,)),
-            dma(()),
-            dma(()),
-            dma(()),
-            dma(()),
-            dma(()),
             dma((ITERS, GROUPS, WINDOW)),
             dma(()),
         ],

time: 63.4 us -> 63.8 us (level)
  no operation moved by 1% of the time
where the time goes in v6:
time: 63.8 us; the launch traced here: 63.7 us
  Pallas kernels  62.3 us (98%)
  local copies, waits for them, and re-layouts  1.32 us (2%)
    pallas_call x1, Pallas kernels, local(): pl.pallas_call(kernel, out_shape=jax.ShapeDtypeStruct(vectors.shape, BF16...  62.3 us
    unnamed x9, local copies, waits for them, and re-layouts  1.32 us

profile of v6, /device:TPU:6, one launch (start us, length us, event | category | flops | bytes accessed | tf_op | source)
XLA Modules:
  0.0 63.7 jit_solution(2399015862111493597)
XLA Ops:
  0.0 0.0 copy-start.3
  0.0 0.0 copy-start
  0.0 0.0 copy-start.1
  0.0 0.0 copy-start.2
  0.0 0.6 copy-done.3
  0.7 0.0 copy-done
  0.7 0.0 copy-done.1
  0.7 0.0 copy-done.2
  0.7 62.3 %shard_map.64 = bf16[6,4096]{1,0:T(8,128)(2,1)S(1)} custom-call(bf16[32,4096]{1,0:T(8,128)(2,1)} %tiles_ref.1, s32[1,32]{1,0:T(1,128)S(1)} %bitcast.4, s32[1,32]{1,0:T(1,128)S(1)} %bitcast.5, s32[1,2]{1,0:T(1,128)S(1)} %bitcast.6, bf16[6,4096]{1,0:T(8,128)(2,1)} %vec_ref.1, f32[1,5]{1,0:T(1,128)S(1)} %bitcast.7), custom_call_target="tpu_custom_call" | custom-call | tf_op jit(solution)/shard_map/pallas_call | solution.py:412
  63.0 0.6 copy.8
Async XLA Ops:
  0.0 0.7 %copy-start.3 = (f32[5]{0:T(128)S(1)}, f32[5]{0:T(128)}, u32[]{:S(2)}) copy-start(f32[5]{0:T(128)} %param.11) | copy-start | bytes 64
  0.0 0.7 %copy-start = (s32[32]{0:T(128)S(1)}, s32[32]{0:T(128)}, u32[]{:S(2)}) copy-start(s32[32]{0:T(128)} %param.7) | copy-start | bytes 388
  0.0 0.7 %copy-start.1 = (s32[32]{0:T(128)S(1)}, s32[32]{0:T(128)}, u32[]{:S(2)}) copy-start(s32[32]{0:T(128)} %param.8) | copy-start | bytes 388
  0.0 0.7 %copy-start.2 = (s32[2]{0:T(128)S(1)}, s32[2]{0:T(128)}, u32[]{:S(2)}) copy-start(s32[2]{0:T(128)} %param.9) | copy-start | bytes 28
